TPU v7x, 256 devices: a whole 4x4x8 slice. The times are simulated.
256 devices in a mesh: seq: 64 (over z, x, y_lo), dp: 4 (over y_hi, core).
Axes of the slice: x: 4, y: 4 (y_hi: 2, y_lo: 2; y = y_hi * 2 + y_lo), z: 8, core: 2. Of those that a mesh axis runs over, the one named last changes fastest.
Arguments:
- tokens: bfloat16 [4, 65536, 512], P('dp', 'seq'), may hold values from -40 to 40
- cotangent: bfloat16 [4, 65536, 512], P('dp', 'seq'), may hold values from -16 to 16
- norm_gain: float32 [512], replicated, may hold values from 0.1 to 1.9
- gate_weight: float32 [512], replicated, may hold values from -4 to 4
- gate_bias: float32 [512], replicated, may hold values from -4 to 4
- first_factor: bfloat16 [512, 128, 128], P('seq'), may hold values from -0.5 to 0.5
- second_factor: bfloat16 [128, 4, 128, 128], P('seq'), may hold values from -0.5 to 0.5
- third_factor: bfloat16 [128, 4, 4, 128], P('seq'), may hold values from -3 to 3
- mlp_gain: float32 [512], replicated, may hold values from 0.1 to 1.9
- up_weight: bfloat16 [512, 2048], replicated, may hold values from -0.25 to 0.25
- down_weight: bfloat16 [2048, 512], replicated, may hold values from -0.125 to 0.125
Outputs:
- block_out: bfloat16 [4, 65536, 512], P('dp', 'seq')
- grad_tokens: bfloat16 [4, 65536, 512], P('dp', 'seq')
- grad_up: float32 [512, 2048], P(('seq', 'dp'))
- grad_down: float32 [512, 2048], P(('seq', 'dp'))
- grad_first: float32 [512, 128, 128], P('seq')
- grad_second: float32 [128, 4, 128, 128], P('seq')
- grad_third: float32 [128, 4, 4, 128], P('seq')
All inputs are finite; a program needn't handle non-finite values.
Results may differ from a plain program's by a relative error of at most 0.018.
Values may be sent and summed in bfloat16 or wider, within the bound.
No kernel may reach another device: no remote copies, remote signals or barrier semaphores. Data moves between devices by JAX's collectives and lax.ppermute only.
A program may use at most 128 MiB of HBM per device.

v0:
```python
import jax
import jax.numpy as jnp
from jax import lax
from jax.sharding import PartitionSpec as P

epsilon = 1e-06


def normalize(values, gain):
    inverse = lax.rsqrt(jnp.mean(values * values, axis=-1, keepdims=True) + epsilon)
    unit_part = values * inverse
    return (unit_part * gain, unit_part, inverse)


def norm_back(grad_in, unit_part, inverse, gain):
    scaled_grad = grad_in * gain
    return inverse * (
        scaled_grad - unit_part * jnp.mean(scaled_grad * unit_part, axis=-1, keepdims=True)
    )


def gelu_tanh(values):
    return jax.nn.gelu(values, approximate=True)


def local(
    tokens,
    cotangent,
    norm_gain,
    gate_weight,
    gate_bias,
    first_factor,
    second_factor,
    third_factor,
    mlp_gain,
    up_weight,
    down_weight,
):
    f32 = jnp.float32
    bf16 = jnp.bfloat16
    sequences, position_count, channels = tokens.shape
    block_rows = first_factor.shape[0]
    cell_count = first_factor.shape[1]
    slice_count, group_count, inner_count = (
        second_factor.shape[0],
        second_factor.shape[1],
        second_factor.shape[2],
    )
    total_rows = sequences * position_count
    tokens_flat = tokens.reshape(total_rows, channels).astype(f32)
    normed, unit_one, inverse_one = normalize(tokens_flat, norm_gain)
    mixer_in = normed.astype(bf16)
    input_grid = mixer_in.reshape(sequences, block_rows, cell_count, channels)
    first_out = jnp.einsum(
        "kpc,zkcd->zkpd", first_factor, input_grid, preferred_element_type=f32
    ).astype(bf16)
    block_in = lax.all_to_all(first_out, "seq", split_axis=2, concat_axis=1, tiled=True)
    layout = block_in.shape
    cube = block_in.reshape(sequences, group_count, inner_count, slice_count, layout[-1])
    second_out = jnp.einsum(
        "caqb,zabcd->zaqcd", second_factor, cube, preferred_element_type=f32
    ).astype(bf16)
    third_out = jnp.einsum(
        "cqab,zabcd->zqbcd", third_factor, second_out, preferred_element_type=f32
    ).astype(bf16)
    cols_first = block_in
    cols_second = second_out.reshape(layout)
    cols_third = third_out.reshape(layout)
    mixed_rows = lax.all_to_all(cols_third, "seq", split_axis=1, concat_axis=2, tiled=True)
    mixed = mixed_rows.reshape(total_rows, channels).astype(f32)
    gate_value = jax.nn.sigmoid(normed * gate_weight + gate_bias)
    hidden = (tokens_flat + gate_value * mixed).astype(bf16)
    hidden_wide = hidden.astype(f32)
    scaled, unit_two, inverse_two = normalize(hidden_wide, mlp_gain)
    scaled = scaled.astype(bf16)
    before = jnp.dot(scaled, up_weight, preferred_element_type=f32)
    act_value, act_back = jax.vjp(gelu_tanh, before)
    active = act_value.astype(bf16)
    block_out = (hidden_wide + jnp.dot(active, down_weight, preferred_element_type=f32)).astype(
        bf16
    )
    back_flat = cotangent.reshape(total_rows, channels)
    through = lax.dot_general(
        back_flat, down_weight, (((1,), (1,)), ((), ())), preferred_element_type=f32
    )
    grad_pre = act_back(through)[0].astype(bf16)
    grad_scaled = lax.dot_general(
        grad_pre, up_weight, (((1,), (1,)), ((), ())), preferred_element_type=f32
    )
    grad_hidden = back_flat.astype(f32) + norm_back(grad_scaled, unit_two, inverse_two, mlp_gain)
    sliced = back_flat
    grad_down = lax.psum_scatter(
        lax.dot_general(sliced, active, (((0,), (0,)), ((), ())), preferred_element_type=f32),
        ("seq", "dp"),
        scatter_dimension=0,
        tiled=True,
    )
    sliced = scaled
    grad_up = lax.psum_scatter(
        lax.dot_general(sliced, grad_pre, (((0,), (0,)), ((), ())), preferred_element_type=f32),
        ("seq", "dp"),
        scatter_dimension=0,
        tiled=True,
    )
    grad_mixed = (grad_hidden * gate_value).astype(bf16)
    gate_term = grad_hidden * mixed * gate_value * (1.0 - gate_value) * gate_weight
    grad_grid = grad_mixed.reshape(sequences, block_rows, cell_count, channels)
    block_in = lax.all_to_all(grad_grid, "seq", split_axis=2, concat_axis=1, tiled=True)
    layout = block_in.shape
    cube = block_in.reshape(sequences, group_count, inner_count, slice_count, layout[-1])
    back_second = jnp.einsum(
        "cqab,zqbcd->zabcd", third_factor, cube, preferred_element_type=f32
    ).astype(bf16)
    back_first = jnp.einsum(
        "caqb,zaqcd->zabcd", second_factor, back_second, preferred_element_type=f32
    ).astype(bf16)
    cols_back_second = back_second.reshape(layout)
    cols_back_first = back_first.reshape(layout)
    cube_layout = (sequences, group_count, inner_count, slice_count, channels)
    grad_third = jnp.einsum(
        "zqbcd,zabcd->cqab",
        block_in.reshape(cube_layout),
        cols_second.reshape(cube_layout),
        preferred_element_type=f32,
    )
    grad_second = jnp.einsum(
        "zaqcd,zabcd->caqb",
        cols_back_second.reshape(cube_layout),
        cols_first.reshape(cube_layout),
        preferred_element_type=f32,
    )
    back_rows = lax.all_to_all(cols_back_first, "seq", split_axis=1, concat_axis=2, tiled=True)
    grad_first = jnp.einsum("zkpd,zkcd->kpc", back_rows, input_grid, preferred_element_type=f32)
    back_input = jnp.einsum(
        "kpc,zkpd->zkcd", first_factor, back_rows, preferred_element_type=f32
    ).reshape(total_rows, channels)
    grad_normed = back_input + gate_term
    grad_tokens = (grad_hidden + norm_back(grad_normed, unit_one, inverse_one, norm_gain)).astype(
        bf16
    )
    grad_first, grad_second, grad_third = (
        lax.psum(grad_first.astype(jnp.bfloat16), "dp").astype(jnp.float32),
        lax.psum(grad_second.astype(jnp.bfloat16), "dp").astype(jnp.float32),
        lax.psum(grad_third.astype(jnp.bfloat16), "dp").astype(jnp.float32),
    )
    return (
        block_out.reshape(tokens.shape),
        grad_tokens.reshape(tokens.shape),
        grad_up,
        grad_down,
        grad_first,
        grad_second,
        grad_third,
    )


def solution(mesh):
    in_specs = (
        P("dp", "seq", None),
        P("dp", "seq", None),
        P(),
        P(),
        P(),
        P("seq", None, None),
        P("seq", None, None, None),
        P("seq", None, None, None),
        P(),
        P(),
        P(),
    )
    out_specs = (
        P("dp", "seq", None),
        P("dp", "seq", None),
        P(("seq", "dp"), None),
        P(("seq", "dp"), None),
        P("seq", None, None),
        P("seq", None, None, None),
        P("seq", None, None, None),
    )
    return jax.shard_map(local, mesh=mesh, in_specs=in_specs, out_specs=out_specs, check_vma=False)
```

profile of v0, /device:TPU:1, one launch (start us, length us, event | category | flops | bytes accessed | tf_op | source)
XLA Modules:
  0.0 495.7 jit_solution(12495107816043501228)
XLA Ops:
  8.8 2.0 fusion.20
  12.6 13.6 %all-to-all-start = ((bf16[1,8,128,512]{3,1,0,2:T(8,128)(2,1)}), bf16[1,8,128,512]{3,1,0,2:T(8,128)(2,1)S(1)}, u32[]{:S(2)}, u32[]{:S(2)}) async-start(bf16[1,8,128,512]{3,1,0,2:T(8,128)(2,1)} %copy.77), calls=%async_computation | async-start | bytes 2097152 | tf_op jit(solution)/shard_map/all_to_all | solution.py:57
  27.1 25.1 %all-to-all-done = bf16[1,8,128,512]{3,1,0,2:T(8,128)(2,1)S(1)} async-done(((bf16[1,8,128,512]{3,1,0,2:T(8,128)(2,1)}), bf16[1,8,128,512]{3,1,0,2:T(8,128)(2,1)S(1)}, u32[]{:S(2)}, u32[]{:S(2)}) %all-to-all-start) | async-done | bytes 1048608 | tf_op jit(solution)/shard_map/all_to_all | solution.py:57
  55.6 2.1 fusion.22
  59.1 33.8 %all_to_all.54 = bf16[1,512,2,512]{3,2,0,1:T(2,128)(2,1)S(1)} all-to-all(bf16[1,512,2,512]{3,2,0,1:T(2,128)(2,1)S(1)} %copy.84), channel_id=1, replica_groups=mesh['seq'=64,'dp'=4] {'seq'}, dimensions={1} | all-to-all | bytes 2097152 | tf_op jit(solution)/shard_map/all_to_all | solution.py:69
  93.2 3.0 copy.86
  96.1 3.8 reshape.156
  99.9 2.9 fusion.15
  102.9 2.4 fusion.37
  105.3 7.4 %fusion.6 = bf16[1024,2048]{1,0:T(8,128)(2,1)S(1)} fusion(f32[1024,2048]{1,0:T(8,128)S(1)} %fusion.37, bf16[2048,512]{1,0:T(8,128)(2,1)S(1)} %copy-done.25, bf16[1,1024,512]{2,1,0:T(8,128)(2,1)S(1)} %copy-done.7), kind=kOutput, calls=%fused_computation.8 | convolution fusion | flops 2189426688 | bytes 15728640 | tf_op jit(solution)/shard_map/dot_general | solution.py:83
  112.8 2.5 fusion.11
  118.5 8.2 %all-to-all-start.2 = ((bf16[1,8,128,512]{3,1,0,2:T(8,128)(2,1)}), bf16[1,8,128,512]{3,1,0,2:T(8,128)(2,1)}, u32[]{:S(2)}, u32[]{:S(2)}) async-start(bf16[1,8,128,512]{3,1,0,2:T(8,128)(2,1)} %copy.87), calls=%async_computation.2 | async-start | bytes 2097152 | tf_op jit(solution)/shard_map/all_to_all | solution.py:108
  126.7 6.8 %fusion.35 = f32[512,2048]{1,0:T(8,128)} fusion(bf16[1024,2048]{1,0:T(8,128)(2,1)} %copy-done.10, bf16[1024,512]{1,0:T(8,128)(2,1)S(1)} %copy-done.4, f32[512]{0:T(512)S(1)} %copy-done.20, f32[1024]{0:T(1024)S(1)} %add_rsqrt_fusion), kind=kOutput, calls=%fused_computation.61 | convolution fusion | flops 2149580800 | bytes 9443328 | tf_op jit(solution)/shard_map/dot_general | solution.py:100
  133.6 4.7 convolution_bitcast_fusion
  138.3 13.5 %all-to-all-done.2 = bf16[1,8,128,512]{3,1,0,2:T(8,128)(2,1)} async-done(((bf16[1,8,128,512]{3,1,0,2:T(8,128)(2,1)}), bf16[1,8,128,512]{3,1,0,2:T(8,128)(2,1)}, u32[]{:S(2)}, u32[]{:S(2)}) %all-to-all-start.2) | async-done | bytes 1048608 | tf_op jit(solution)/shard_map/all_to_all | solution.py:108
  155.2 2.0 copy.94
  157.2 8.5 %all-to-all-start.3 = ((bf16[1,512,2,512]{3,2,0,1:T(2,128)(2,1)}), bf16[1,512,2,512]{3,2,0,1:T(2,128)(2,1)}, u32[]{:S(2)}, u32[]{:S(2)}) async-start(bf16[1,512,2,512]{3,2,0,1:T(2,128)(2,1)} %copy.94), calls=%async_computation.3 | async-start | bytes 2097152 | tf_op jit(solution)/shard_map/all_to_all | solution.py:132
  166.1 2.7 copy.99
  168.8 8.1 %fusion.25 = bf16[1,1024,512]{2,1,0:T(8,128)(2,1)} fusion(bf16[2048,512]{1,0:T(8,128)(2,1)} %param.21, bf16[1024,512]{1,0:T(8,128)(2,1)S(1)} %copy-done.4, f32[1024,2048]{1,0:T(8,128)} %copy-done.26), kind=kOutput, calls=%fused_computation.47 | convolution fusion | flops 2167930880 | bytes 12582912 | tf_op jit(solution)/shard_map/dot_general | solution.py:79
  176.9 2.0 fusion.26
  178.8 22.1 %psum.23 = bf16[2,4,4,128]{1,2,3,0:T(4,128)(2,1)S(1)} all-reduce(bf16[2,4,4,128]{1,2,3,0:T(4,128)(2,1)} %fusion.26), channel_id=1, replica_groups=mesh['seq'=64,'dp'=4] {'dp'}, use_global_device_ids=true, to_apply=%region_8.0 | all-reduce | flops 4096 | bytes 16384 | tf_op jit(solution)/shard_map/psum | solution.py:144
  201.7 2.8 convolution_convert_fusion.6
  206.0 2.0 copy.96
  208.0 2.3 reshape.151
  210.3 1.9 fusion.46
  212.2 4.6 multiply_reduce_fusion
  218.1 3.6 fusion.34
  221.8 211.9 %all-reduce.7.cloned.1.call-done = (f32[512,2048]{1,0:T(8,128)}, f32[512,2048]{0,1:T(8,128)}) async-done(((f32[512,2048]{1,0:T(8,128)}, f32[512,2048]{0,1:T(8,128)}), (f32[512,2048]{1,0:T(8,128)}, f32[512,2048]{0,1:T(8,128)})) %all-reduce.7.cloned.1.call-update) | async-done | bytes 8388624
  433.6 1.7 constant_dynamic-slice_fusion
  437.7 47.2 %all-reduce.9.cloned.1.call-done = (bf16[8,128,128]{2,1,0:T(8,128)(2,1)}, bf16[2,4,128,128]{3,2,1,0:T(8,128)(2,1)}) async-done(((bf16[8,128,128]{2,1,0:T(8,128)(2,1)}, bf16[2,4,128,128]{3,2,1,0:T(8,128)(2,1)}), (bf16[8,128,128]{2,1,0:T(8,128)(2,1)}, bf16[2,4,128,128]{3,2,1,0:T(8,128)(2,1)})) %all-reduce.9.cloned.1.call-update) | async-done | bytes 524304 | tf_op jit(solution)/shard_map/psum | solution.py:142
  484.9 1.8 convert_element_type.159
  486.7 1.8 convert_element_type.161
  (85 shorter events, 22.1 us)
Async XLA Ops:
  7.2 95.7 %copy-start = (bf16[512,2048]{1,0:T(8,128)(2,1)S(1)}, bf16[512,2048]{1,0:T(8,128)(2,1)}, u32[]{:S(2)}) copy-start(bf16[512,2048]{1,0:T(8,128)(2,1)} %param.20) | copy-start | bytes 6291460
  10.9 15.3 %copy-start.24 = (bf16[2,4,4,128]{3,2,1,0:T(4,128)(2,1)S(1)}, bf16[2,4,4,128]{3,2,1,0:T(4,128)(2,1)}, u32[]{:S(2)}) copy-start(bf16[2,4,4,128]{3,2,1,0:T(4,128)(2,1)} %param.18) | copy-start | bytes 24580
  12.6 40.8 %copy-start.13 = (bf16[2,4,128,128]{3,2,1,0:T(8,128)(2,1)S(1)}, bf16[2,4,128,128]{3,2,1,0:T(8,128)(2,1)}, u32[]{:S(2)}) copy-start(bf16[2,4,128,128]{3,2,1,0:T(8,128)(2,1)} %param.17) | copy-start | bytes 786436
  12.6 39.7 %all-to-all-start = ((bf16[1,8,128,512]{3,1,0,2:T(8,128)(2,1)}), bf16[1,8,128,512]{3,1,0,2:T(8,128)(2,1)S(1)}, u32[]{:S(2)}, u32[]{:S(2)}) async-start(bf16[1,8,128,512]{3,1,0,2:T(8,128)(2,1)} %copy.77), calls=%async_computation | async-start | bytes 2097152 | tf_op jit(solution)/shard_map/all_to_all | solution.py:57
  52.3 1.0 copy-start.11
  53.9 3.8 copy-start.9
  96.1 3.8 copy-start.2
  96.1 3.8 copy-start.21
  96.1 3.8 copy-start.22
  96.1 3.8 copy-start.23
  99.9 3.0 copy-start.20
  102.8 12.5 %copy-start.3 = (bf16[1024,512]{1,0:T(8,128)(2,1)}, bf16[1024,512]{1,0:T(8,128)(2,1)S(1)}, u32[]{:S(2)}) copy-start(bf16[1024,512]{1,0:T(8,128)(2,1)S(1)} %get-tuple-element.42) | copy-start | bytes 3145732
  102.9 2.4 copy-start.7
  102.9 2.4 copy-start.25
  105.3 7.4 %copy-start.26 = (f32[1024,2048]{1,0:T(8,128)}, f32[1024,2048]{1,0:T(8,128)S(1)}, u32[]{:S(2)}) copy-start(f32[1024,2048]{1,0:T(8,128)S(1)} %fusion.37) | copy-start | bytes 25165828
  112.7 2.5 copy-start.10
  115.3 1.6 copy-start.5
  116.9 9.8 %copy-start.4 = (bf16[1024,512]{1,0:T(8,128)(2,1)S(1)}, bf16[1024,512]{1,0:T(8,128)(2,1)}, u32[]{:S(2)}) copy-start(bf16[1024,512]{1,0:T(8,128)(2,1)} %copy-done.3) | copy-start | bytes 3145732
  118.5 33.3 %all-to-all-start.2 = ((bf16[1,8,128,512]{3,1,0,2:T(8,128)(2,1)}), bf16[1,8,128,512]{3,1,0,2:T(8,128)(2,1)}, u32[]{:S(2)}, u32[]{:S(2)}) async-start(bf16[1,8,128,512]{3,1,0,2:T(8,128)(2,1)} %copy.87), calls=%async_computation.2 | async-start | bytes 2097152 | tf_op jit(solution)/shard_map/all_to_all | solution.py:108
  126.7 6.9 %copy-start.8 = (bf16[1,1024,512]{2,1,0:T(8,128)(2,1)S(1)}, bf16[1,1024,512]{2,1,0:T(8,128)(2,1)}, u32[]{:S(2)}) copy-start(bf16[1,1024,512]{2,1,0:T(8,128)(2,1)} %param.12) | copy-start | bytes 3145732
  126.7 306.9 %all-reduce.7.cloned.1.call-start = ((), (), s32[]{:S(2)}) async-start(), calls=%async_computation.4 | async-start | bytes 16777216
  126.7 6.8 %copy-start.27 = (f32[1024,2048]{1,0:T(8,128)S(1)}, f32[1024,2048]{1,0:T(8,128)}, u32[]{:S(2)}) copy-start(f32[1024,2048]{1,0:T(8,128)} %copy-done.26) | copy-start | bytes 25165828
  151.8 1.4 copy-start.19
  153.2 1.9 copy-start.15
  157.2 47.3 %all-to-all-start.3 = ((bf16[1,512,2,512]{3,2,0,1:T(2,128)(2,1)}), bf16[1,512,2,512]{3,2,0,1:T(2,128)(2,1)}, u32[]{:S(2)}, u32[]{:S(2)}) async-start(bf16[1,512,2,512]{3,2,0,1:T(2,128)(2,1)} %copy.94), calls=%async_computation.3 | async-start | bytes 2097152 | tf_op jit(solution)/shard_map/all_to_all | solution.py:132
  165.8 319.1 %all-reduce.9.cloned.1.call-start = ((), (), s32[]{:S(2)}) async-start(), calls=%async_computation.5 | async-start | bytes 1048576 | tf_op jit(solution)/shard_map/psum | solution.py:142
  168.8 8.1 %copy-start.16 = (bf16[1,64,8,2,512]{4,2,1,3,0:T(8,128)(2,1)S(1)}, bf16[1,64,8,2,512]{4,2,1,3,0:T(8,128)(2,1)}, u32[]{:S(2)}) copy-start(bf16[1,64,8,2,512]{4,2,1,3,0:T(8,128)(2,1)} %copy-done.15) | copy-start | bytes 3145732
  168.8 8.1 %copy-start.17 = (bf16[4,128,2,512]{3,0,1,2:T(4,128)(2,1)S(1)}, bf16[4,128,2,512]{3,0,1,2:T(4,128)(2,1)}, u32[]{:S(2)}) copy-start(bf16[4,128,2,512]{3,0,1,2:T(4,128)(2,1)} %copy.99) | copy-start | bytes 3145732
  205.9 4.3 copy-start.18
  210.3 1.9 copy-start.6
  212.2 4.6 copy-start.12
  433.6 54.8 %copy-start.1 = (bf16[512,2048]{1,0:T(8,128)(2,1)S(1)}, bf16[512,2048]{1,0:T(8,128)(2,1)}, u32[]{:S(2)}) copy-start(bf16[512,2048]{1,0:T(8,128)(2,1)} %param.20) | copy-start | bytes 6291460
  (1 other events, 1.0 us)
Sparse Core Ops, SparseCore 0:
  138.4 295.1 all-reduce.6
  437.1 47.7 all-reduce.8
where the time goes:
time: 502 us; the launch traced here: 496 us
  waiting for transfers between devices  298 us (59%)
  blocking collectives  55.9 us (11%)
  matrix products  46.3 us (9%)
  local copies, waits for them, and re-layouts  32 us (6%)
  starting transfers between devices  30.7 us (6%)
  other arithmetic  18.2 us (4%)
  between operations  14.9 us (3%)
    unnamed x3, waiting for transfers between devices  212 us
    psum x1, waiting for transfers between devices, local(): lax.psum(grad_first.astype(jnp.bfloat16), 'dp').astype(jnp.float32)  47.2 us
    all_to_all x1, blocking collectives, local(): lax.all_to_all(cols_third, 'seq', split_axis=1, concat_axis=2, tiled=True)  33.8 us
    all_to_all x1, waiting for transfers between devices, local(): lax.all_to_all(first_out, 'seq', split_axis=2, concat_axis=1, tiled=True)  25.1 us
    psum x1, blocking collectives, local(): lax.psum(grad_third.astype(jnp.bfloat16), 'dp').astype(jnp.float32)  22.1 us
    all_to_all x1, starting transfers between devices, local(): lax.all_to_all(first_out, 'seq', split_axis=2, concat_axis=1, tiled=True)  13.6 us
    all_to_all x1, waiting for transfers between devices, local(): lax.all_to_all(grad_grid, 'seq', split_axis=2, concat_axis=1, tiled=True)  13.5 us
  transfers between devices with their start and end apart: 5, of which 4 were waited for; matrix products, arithmetic and copies ran while one was open for 11% of the time, Pallas kernels for 0%

commit v1 on v0

v1 whole, which is shorter than its diff:
```python
import jax
import jax.numpy as jnp
from jax import lax
from jax.experimental import pallas as pl
from jax.experimental.pallas import tpu as pltpu
from jax.sharding import PartitionSpec as P

f32 = jnp.float32
bf16 = jnp.bfloat16
epsilon = 1e-06
D = 512
FF = 2048
TILE = 512
GELU_SCALE = 0.7978845608028654
GELU_CUBE = 0.044715


def nn(a, b):
    return lax.dot_general(a, b, (((1,), (0,)), ((), ())), preferred_element_type=f32)


def nt(a, b):
    return lax.dot_general(a, b, (((1,), (1,)), ((), ())), preferred_element_type=f32)


def tn(a, b):
    return lax.dot_general(a, b, (((0,), (0,)), ((), ())), preferred_element_type=f32)


def iota(shape, dim):
    return lax.broadcasted_iota(jnp.int32, shape, dim)


def one_where(mask):
    return jnp.where(mask, 1.0, 0.0).astype(bf16)


def split_digit():
    row, col = iota((128, 128), 0), iota((128, 128), 1)
    return one_where(col == 2 * (row % 64) + row // 64)


def merge_digit():
    row, col = iota((128, 128), 0), iota((128, 128), 1)
    return one_where(row == 2 * (col % 64) + col // 64)


def spread_digit(e):
    row, col = iota((128, 256), 0), iota((128, 256), 1)
    return one_where((row == (col // 16) * 8 + col % 8) & ((col % 16) // 8 == e))


def inverse_of(values):
    return lax.rsqrt(jnp.mean(values * values, axis=-1, keepdims=True) + epsilon)


def norm_back(grad_in, unit_part, inverse, gain):
    scaled_grad = grad_in * gain
    return inverse * (
        scaled_grad - unit_part * jnp.mean(scaled_grad * unit_part, axis=-1, keepdims=True)
    )


def rows_of(k, size=128):
    return slice(k * size, (k + 1) * size)


def put_wire(wide_ref, k, values):
    for e in range(2):
        for lane in range(4):
            wide_ref[lane, pl.ds(e * 8 + k, 64, 16), :] = values[rows_of(e, 64), rows_of(lane)]


def get_wire(wide_ref, k):
    lanes = [
        jnp.concatenate([wide_ref[lane, pl.ds(e * 8 + k, 64, 16), :] for e in range(2)], axis=0)
        for lane in range(4)
    ]
    return jnp.concatenate(lanes, axis=1)


def to_wide(wide_ref, wire_ref):
    for lane in range(4):
        wide_ref[lane] = wire_ref[:, rows_of(lane)].astype(f32)


def from_wide(wire_ref, wide_ref):
    for lane in range(4):
        wire_ref[:, rows_of(lane)] = wide_ref[lane].astype(bf16)


WIDE = pltpu.VMEM((4, 1024, 128), f32)
PAIR = 2
PART = 256


def first_kernel(tokens_ref, gain_ref, factor_ref, wire_ref, wide_ref):
    step = pl.program_id(0)
    split = split_digit()
    for k in range(PAIR):
        values = tokens_ref[rows_of(k)].astype(f32)
        normed = values * inverse_of(values) * gain_ref[...]
        factor = nn(split, factor_ref[k]).astype(bf16)
        put_wire(wide_ref, step * PAIR + k, nn(factor, normed.astype(bf16)))

    @pl.when(step == pl.num_programs(0) - 1)
    def _():
        from_wide(wire_ref, wide_ref)


def gate_kernel(tokens_ref, gain_ref, weight_ref, bias_ref, gate_ref, input_ref):
    values = tokens_ref[...].astype(f32)
    normed = values * inverse_of(values) * gain_ref[...]
    input_ref[...] = normed.astype(bf16)
    gate = 0.5 + 0.5 * jnp.tanh(0.5 * (normed * weight_ref[...] + bias_ref[...]))
    gate_ref[...] = gate.astype(bf16)


def prepare_kernel(second_ref, third_ref, wide_factor_ref, columns_ref):
    spreads = [spread_digit(e) for e in range(2)]
    for a in range(4):
        total = jnp.zeros((256, 256), f32)
        for e in range(2):
            part = nn(second_ref[e, a], spreads[e]).astype(bf16)
            total = total + tn(spreads[e], part)
        wide_factor_ref[a] = total.astype(bf16)
    columns_ref[...] = tn(spreads[0], third_ref[0]) + tn(spreads[1], third_ref[1])


def mix_kernel(first_ref, factor_ref, columns_ref, second_ref, wire_ref):
    for a in range(4):
        rows = rows_of(a, 256)
        second_ref[rows] = nn(factor_ref[a], first_ref[rows]).astype(bf16)
    for q in range(4):
        total = None
        for a in range(4):
            index = q * 4 + a
            term = columns_ref[:, index : index + 1] * second_ref[rows_of(a, 256)].astype(f32)
            total = term if total is None else total + term
        wire_ref[rows_of(q, 256)] = total.astype(bf16)


def unmix_kernel(
    grad_ref, factor_ref, columns_ref, core_token_ref, second_ref, wire_ref, token_ref
):
    token_ref[...] = jnp.zeros_like(token_ref)
    for a in range(4):
        rows = rows_of(a, 256)
        total = None
        for q in range(4):
            index = q * 4 + a
            term = columns_ref[:, index : index + 1] * grad_ref[rows_of(q, 256)].astype(f32)
            total = term if total is None else total + term
        second = total.astype(bf16)
        second_ref[rows] = second
        wire_ref[rows] = tn(factor_ref[a], second).astype(bf16)


def factor_grad_kernel(grad_ref, second_ref, first_ref, back_ref, out_ref, token_ref):
    token_ref[...] = jnp.zeros_like(token_ref)
    spreads = [spread_digit(e) for e in range(2)]
    lane = iota((256, 128), 1)
    sums = jnp.zeros((256, 128), f32)
    for q in range(4):
        grad = grad_ref[rows_of(q, 256)].astype(f32)
        for a in range(4):
            product = grad * second_ref[rows_of(a, 256)].astype(f32)
            sums = jnp.where(lane == q * 4 + a, jnp.sum(product, axis=-1, keepdims=True), sums)
    sums = sums.astype(bf16)
    for e in range(2):
        out_ref[1024 + e * 16 : 1040 + e * 16] = tn(sums, spreads[e].T)[0:16].astype(bf16)
    for a in range(4):
        rows = rows_of(a, 256)
        wide = nt(back_ref[rows], first_ref[rows]).astype(bf16)
        for e in range(2):
            part = nn(spreads[e], wide).astype(bf16)
            out_ref[rows_of(e * 4 + a)] = nt(part, spreads[e]).astype(bf16)


def mlp_kernel(
    tokens_ref,
    cot_ref,
    wire_ref,
    gate_ref,
    through_ref,
    mlp_gain_ref,
    up_ref,
    hidden_ref,
    active_ref,
    grad_pre_ref,
    grad_hidden_ref,
    out_ref,
    wide_ref,
    scaled_ref,
    total_ref,
):
    step = pl.program_id(0)

    @pl.when(step == 0)
    def _():
        to_wide(wide_ref, wire_ref)
        merge = merge_digit()
        for k in range(8):
            rows = rows_of(k)
            mixed = nn(merge, get_wire(wide_ref, k).astype(bf16))
            gated = gate_ref[rows].astype(f32) * mixed
            hidden = (tokens_ref[rows].astype(f32) + gated).astype(bf16)
            hidden_ref[rows] = hidden
            hidden = hidden.astype(f32)
            scaled_ref[rows] = (hidden * inverse_of(hidden) * mlp_gain_ref[...]).astype(bf16)
        total_ref[...] = jnp.zeros_like(total_ref)

    up = up_ref[...]
    for part in range(1024 // PART):
        rows = rows_of(part, PART)
        value = nn(scaled_ref[rows], up)
        square = value * value
        tanh = jnp.tanh(value * (GELU_SCALE + (GELU_SCALE * GELU_CUBE) * square))
        outer = 0.5 + 0.5 * tanh
        active = value * outer
        slope = outer + active * (1.0 - outer) * (
            2.0 * GELU_SCALE + (6.0 * GELU_SCALE * GELU_CUBE) * square
        )
        active_ref[rows] = active.astype(bf16)
        grad_pre = (through_ref[rows].astype(f32) * slope).astype(bf16)
        grad_pre_ref[rows] = grad_pre
        total_ref[rows] += nt(grad_pre, up)

    @pl.when(step == pl.num_programs(0) - 1)
    def _():
        split = split_digit()
        for k in range(8):
            rows = rows_of(k)
            hidden = hidden_ref[rows].astype(f32)
            inverse = inverse_of(hidden)
            grad_hidden = cot_ref[rows].astype(f32) + norm_back(
                total_ref[rows], hidden * inverse, inverse, mlp_gain_ref[...]
            )
            grad_hidden_ref[rows] = grad_hidden.astype(bf16)
            gated = grad_hidden * gate_ref[rows].astype(f32)
            put_wire(wide_ref, k, nn(split, gated.astype(bf16)))
        from_wide(out_ref, wide_ref)


def owner_rows(place_ref):
    row, col = iota((512, 512), 0), iota((512, 512), 1)
    core = (row // 256 + place_ref[0]) % 2
    y = (row // 64 + place_ref[1]) % 4
    x = (row // 16 + place_ref[2]) % 4
    z = ((row // 2) % 8) ^ place_ref[3]
    return one_where(col == z * 64 + x * 16 + (y % 2) * 8 + (y // 2) * 4 + core * 2 + row % 2)


def through_kernel(place_ref, cot_ref, down_ref, through_ref, cot_t_ref):
    through_ref[...] = nt(cot_ref[...], down_ref[...]).astype(bf16)

    @pl.when(pl.program_id(0) == 0)
    def _():
        cot_t_ref[...] = nt(owner_rows(place_ref), cot_ref[...]).astype(bf16)


def weight_grad_kernel(
    place_ref,
    cot_t_ref,
    hidden_ref,
    mlp_gain_ref,
    active_ref,
    grad_pre_ref,
    keep_ref,
    send_up_ref,
    send_down_ref,
    scaled_t_ref,
):
    @pl.when(pl.program_id(0) == 0)
    def _():
        owner = owner_rows(place_ref)
        for part in range(4):
            rows = rows_of(part, 256)
            hidden = hidden_ref[rows].astype(f32)
            scaled = (hidden * inverse_of(hidden) * mlp_gain_ref[...]).astype(bf16)
            scaled_t_ref[:, rows] = nt(owner, scaled).astype(bf16)

    for index, (left_ref, right_ref, send_ref) in enumerate(
        ((scaled_t_ref, grad_pre_ref, send_up_ref), (cot_t_ref, active_ref, send_down_ref))
    ):
        keep_ref[index] = nn(left_ref[0:256], right_ref[...]).astype(bf16)
        send_ref[...] = nn(left_ref[256:512], right_ref[...]).astype(bf16)


def gate_term_kernel(
    wire_ref, gate_ref, gate_weight_ref, grad_hidden_ref, order_ref, term_ref, token_ref, wide_ref
):
    step = pl.program_id(0)

    @pl.when(step == 0)
    def _():
        to_wide(wide_ref, wire_ref)
        token_ref[...] = jnp.zeros_like(token_ref)

    merge = merge_digit()
    for k in range(PAIR):
        rows = rows_of(k)
        mixed = nn(merge, get_wire(wide_ref, step * PAIR + k).astype(bf16))
        gate = gate_ref[rows].astype(f32)
        slope = gate * (1.0 - gate) * gate_weight_ref[...]
        term_ref[rows] = grad_hidden_ref[rows].astype(f32) * mixed * slope


def first_grad_kernel(
    wire_ref, input_ref, factor_order_ref, term_order_ref, out_order_ref, out_ref, wide_ref
):
    step = pl.program_id(0)

    @pl.when(step == 0)
    def _():
        to_wide(wide_ref, wire_ref)

    merge = merge_digit()
    for k in range(PAIR):
        grad = get_wire(wide_ref, step * PAIR + k).astype(bf16)
        grad = nt(grad, input_ref[rows_of(k)]).astype(bf16)
        out_ref[rows_of(k)] = nn(merge, grad).astype(bf16)


def token_grad_kernel(
    wire_ref, tokens_ref, gain_ref, factor_ref, grad_hidden_ref, gate_term_ref, out_ref, wide_ref
):
    step = pl.program_id(0)

    @pl.when(step == 0)
    def _():
        to_wide(wide_ref, wire_ref)

    split = split_digit()
    for k in range(PAIR):
        rows = rows_of(k)
        values = tokens_ref[rows].astype(f32)
        inverse = inverse_of(values)
        factor = nn(split, factor_ref[k]).astype(bf16)
        back_input = tn(factor, get_wire(wide_ref, step * PAIR + k).astype(bf16))
        grad_normed = back_input + gate_term_ref[rows]
        out_ref[rows] = (
            grad_hidden_ref[rows].astype(f32)
            + norm_back(grad_normed, values * inverse, inverse, gain_ref[...])
        ).astype(bf16)


def shape(dims, dtype):
    return jax.ShapeDtypeStruct(dims, dtype)


def held(dims, dtype):
    return pltpu.HBM(dims, dtype)


def whole(*dims):
    return pl.BlockSpec(dims, lambda *_: (0,) * len(dims))


def row_blocks(rows, cols=D):
    return pl.BlockSpec((rows, cols), lambda i: (i, 0))


def col_blocks(rows, cols):
    return pl.BlockSpec((rows, cols), lambda i: (0, i))


def call(kernel, grid, in_specs, out_specs, out_shape, scratch, flops, moved, room):
    return pl.pallas_call(
        kernel,
        grid=(grid,),
        in_specs=in_specs,
        out_specs=out_specs,
        out_shape=out_shape,
        scratch_shapes=scratch,
        cost_estimate=pl.CostEstimate(flops=flops, bytes_accessed=moved, transcendentals=0),
        compiler_params=pltpu.CompilerParams(vmem_limit_bytes=room * 1024 * 1024),
    )


BOTH = ("seq", "dp")
SAME_CHIP = [(0, 1), (1, 0), (2, 3), (3, 2)]
FAR_CHIP = [(0, 2), (2, 0), (1, 3), (3, 1)]


def device_index(z, x, y, core):
    return ((z * 4 + x) * 2 + y % 2) * 4 + (y // 2) * 2 + core


def shift_pairs(axis, amount):
    pairs = []
    for z in range(8):
        for x in range(4):
            for y in range(4):
                for core in range(2):
                    target = {
                        "y": (z, x, (y + amount) % 4, core),
                        "x": (z, (x + amount) % 4, y, core),
                        "z": (z ^ amount, x, y, core),
                    }[axis]
                    pairs.append((device_index(z, x, y, core), device_index(*target)))
    return pairs


def add_parts(*parts):
    total = parts[0].astype(f32)
    for part in parts[1:]:
        total = total + part.astype(f32)
    return total


def core_sum_kernel(keep_ref, up_ref, down_ref, *refs):
    token_ref = refs[-1]
    for matrix, arrived_ref in enumerate((up_ref, down_ref)):
        for index in range(4):
            rows = rows_of(index, 64)
            total = keep_ref[matrix, rows].astype(f32) + arrived_ref[rows].astype(f32)
            refs[index][matrix] = total.astype(bf16)
    token_ref[...] = jnp.zeros_like(token_ref)


def plane_sum_kernel(token_ref, *refs):
    parts, results = refs[:4], refs[4:]
    for index, result_ref in enumerate(results):
        rows = rows_of(index, 16)
        for matrix in range(2):
            total = parts[0][matrix, rows].astype(f32)
            for part in parts[1:]:
                total = total + part[matrix, rows].astype(f32)
            result_ref[matrix] = total.astype(bf16)


def line_sum_kernel(order_ref, *refs):
    parts, results = refs[:-2], refs[-2:]
    rows = results[0].shape[1]
    for matrix in range(2):
        total = parts[0][matrix].astype(f32)
        for part in parts[1:]:
            total = total + part[matrix].astype(f32)
        for index, result_ref in enumerate(results):
            result_ref[matrix] = total[rows_of(index, rows)].astype(bf16)


def line_sum(parts, order):
    rows = parts[0].shape[1]
    return call(
        line_sum_kernel,
        1,
        [pl.BlockSpec(memory_space=pl.ANY)] + [whole(2, rows, FF)] * len(parts),
        [whole(2, rows // 2, FF)] * 2,
        [shape((2, rows // 2, FF), bf16)] * 2,
        [],
        1_000,
        1_000,
        8,
    )(order, *parts)


def send_around(blocks, axis):
    return [blocks[0]] + [
        lax.ppermute(blocks[amount], BOTH, shift_pairs(axis, amount))
        for amount in range(1, len(blocks))
    ]


def sequence_sum(part):
    part = add_parts(part, lax.ppermute(part, "dp", SAME_CHIP)).astype(bf16)
    return add_parts(part, lax.ppermute(part, "dp", FAR_CHIP)).astype(bf16)


def exchange(wire):
    return lax.all_to_all(wire, "seq", split_axis=0, concat_axis=0, tiled=True)


def local(
    tokens,
    cotangent,
    norm_gain,
    gate_weight,
    gate_bias,
    first_factor,
    second_factor,
    third_factor,
    mlp_gain,
    up_weight,
    down_weight,
):
    tokens = tokens.reshape(1024, D)
    cot = cotangent.reshape(1024, D)
    norm_gain, gate_weight, gate_bias, mlp_gain = (
        value.reshape(1, D) for value in (norm_gain, gate_weight, gate_bias, mlp_gain)
    )
    seq, dp = lax.axis_index("seq"), lax.axis_index("dp")
    place = jnp.stack(
        [dp & 1, (dp >> 1) * 2 + (seq & 1), (seq >> 1) & 3, seq >> 3]
    ).astype(jnp.int32)
    place_spec = pl.BlockSpec(memory_space=pltpu.SMEM)
    rows16, rows32 = shape((1024, D), bf16), shape((1024, D), f32)
    full, vector = whole(1024, D), whole(1, D)
    pair_rows = row_blocks(PAIR * 128)
    pair_factor = pl.BlockSpec((PAIR, 128, 128), lambda i: (i, 0, 0))
    steps = 8 // PAIR
    wide_columns = shape((1024, FF), bf16)
    held16, held_token = held((1024, D), bf16), held((16, 128), bf16)
    token_spec, token_shape = whole(16, 128), shape((16, 128), bf16)

    wire = call(
        first_kernel,
        steps,
        [pair_rows, vector, pair_factor],
        full,
        rows16,
        [WIDE],
        140_000_000,
        2_400_000,
        56,
    )(tokens, norm_gain, first_factor)
    first = exchange(wire)

    wide_factor, columns = call(
        prepare_kernel,
        1,
        [whole(2, 4, 128, 128), whole(2, 128, 16)],
        [whole(4, 256, 256), whole(256, 16)],
        [shape((4, 256, 256), bf16), shape((256, 16), f32)],
        [],
        200_000_000,
        1_000_000,
        24,
    )(second_factor, third_factor.reshape(2, 16, 128).transpose(0, 2, 1))
    gate, mixer_in = call(
        gate_kernel,
        4,
        [row_blocks(256), vector, vector, vector],
        [row_blocks(256), row_blocks(256)],
        [rows16, rows16],
        [],
        10_000_000,
        4_000_000,
        56,
    )(tokens, norm_gain, gate_weight, gate_bias)
    through, cot_t = call(
        through_kernel,
        FF // TILE,
        [place_spec, full, row_blocks(TILE)],
        [col_blocks(1024, TILE), whole(D, 1024)],
        [wide_columns, shape((D, 1024), bf16)],
        [],
        2_700_000_000,
        14_000_000,
        56,
    )(place, cot, down_weight)

    second, wire = call(
        mix_kernel,
        2,
        [col_blocks(1024, 256), whole(4, 256, 256), whole(256, 16)],
        [col_blocks(1024, 256), col_blocks(1024, 256)],
        [held16, held16],
        [],
        280_000_000,
        4_000_000,
        24,
    )(first, wide_factor, columns)
    wire = exchange(wire)

    mixed_wire = wire
    hidden, active, grad_pre, grad_hidden, wire = call(
        mlp_kernel,
        FF // TILE,
        [
            full,
            full,
            full,
            full,
            col_blocks(1024, TILE),
            vector,
            col_blocks(D, TILE),
        ],
        [full, col_blocks(1024, TILE), col_blocks(1024, TILE), full, full],
        [rows16, wide_columns, wide_columns, rows16, rows16],
        [WIDE, pltpu.VMEM((1024, D), bf16), pltpu.VMEM((1024, D), f32)],
        4_300_000_000,
        20_000_000,
        56,
    )(tokens, cot, wire, gate, through, mlp_gain, up_weight)
    grad_mixed = exchange(wire)

    keep, send_up, send_down = call(
        weight_grad_kernel,
        FF // TILE,
        [
            place_spec,
            whole(D, 1024),
            full,
            vector,
            col_blocks(1024, TILE),
            col_blocks(1024, TILE),
        ],
        [pl.BlockSpec((2, 256, TILE), lambda i: (0, 0, i))] + [col_blocks(256, TILE)] * 2,
        [shape((2, 256, FF), bf16)] + [shape((256, FF), bf16)] * 2,
        [pltpu.VMEM((D, 1024), bf16)],
        4_800_000_000,
        14_000_000,
        56,
    )(place, cot_t, hidden, mlp_gain, active, grad_pre)
    *blocks, core_token = call(
        core_sum_kernel,
        1,
        [whole(2, 256, FF), whole(256, FF), whole(256, FF)],
        [whole(2, 64, FF)] * 4 + [token_spec],
        [shape((2, 64, FF), bf16)] * 4 + [token_shape],
        [],
        1_000,
        1_000,
        56,
    )(keep, *(lax.ppermute(part, "dp", SAME_CHIP) for part in (send_up, send_down)))
    parts = send_around(blocks, "y")

    back_second, wire, token = call(
        unmix_kernel,
        2,
        [col_blocks(1024, 256), whole(4, 256, 256), whole(256, 16), token_spec],
        [col_blocks(1024, 256), col_blocks(1024, 256), token_spec],
        [held16, held16, held_token],
        [],
        1_000,
        1_000,
        24,
    )(grad_mixed, wide_factor, columns, core_token)
    back = exchange(wire)
    gate_term, term_token = call(
        gate_term_kernel,
        steps,
        [full, pair_rows, vector, pair_rows, token_spec],
        [pair_rows, token_spec],
        [rows32, token_shape],
        [WIDE],
        1_000_000,
        1_000,
        56,
    )(mixed_wire, gate, gate_weight, grad_hidden, token)
    block_out = (hidden.astype(f32) + nn(active, down_weight)).astype(bf16)
    factor_grads, factor_token = call(
        factor_grad_kernel,
        1,
        [full, full, full, full],
        [whole(1056, 128), token_spec],
        [shape((1056, 128), bf16), token_shape],
        [],
        1_000,
        1_000,
        56,
    )(grad_mixed, second, first, back_second)
    factor_grads = sequence_sum(factor_grads)

    blocks = call(
        plane_sum_kernel,
        1,
        [token_spec] + [whole(2, 64, FF)] * 4,
        [whole(2, 16, FF)] * 4,
        [shape((2, 16, FF), bf16)] * 4,
        [],
        1_000_000,
        2_500_000,
        16,
    )(token, *parts)
    parts = send_around(blocks, "x")
    parts = line_sum(parts, wire)
    parts = [parts[0], lax.ppermute(parts[1], BOTH, shift_pairs("z", 4))]
    parts = line_sum(parts, wire)
    parts = [parts[0], lax.ppermute(parts[1], BOTH, shift_pairs("z", 2))]
    parts = line_sum(parts, back)
    parts = [parts[0], lax.ppermute(parts[1], BOTH, shift_pairs("z", 1))]
    weight_grads = add_parts(*parts)

    grad_first = call(
        first_grad_kernel,
        steps,
        [full, pair_rows, token_spec, token_spec, pl.BlockSpec(memory_space=pl.ANY)],
        row_blocks(PAIR * 128, 128),
        shape((1024, 128), bf16),
        [WIDE],
        140_000_000,
        3_000_000,
        24,
    )(back, mixer_in, factor_token, term_token, block_out)
    grad_first = sequence_sum(grad_first)
    grad_tokens = call(
        token_grad_kernel,
        steps,
        [full, pair_rows, vector, pair_factor, pair_rows, pair_rows],
        pair_rows,
        rows16,
        [WIDE],
        140_000_000,
        8_000_000,
        24,
    )(back, tokens, norm_gain, first_factor, grad_hidden, gate_term)

    return (
        block_out.reshape(1, 1024, D),
        grad_tokens.reshape(1, 1024, D),
        weight_grads[0],
        weight_grads[1],
        grad_first.astype(f32).reshape(8, 128, 128),
        factor_grads[:1024].astype(f32).reshape(2, 4, 128, 128),
        factor_grads[1024:].astype(f32).reshape(2, 4, 4, 128),
    )


def solution(mesh):
    in_specs = (
        P("dp", "seq", None),
        P("dp", "seq", None),
        P(),
        P(),
        P(),
        P("seq", None, None),
        P("seq", None, None, None),
        P("seq", None, None, None),
        P(),
        P(),
        P(),
    )
    out_specs = (
        P("dp", "seq", None),
        P("dp", "seq", None),
        P(("seq", "dp"), None),
        P(("seq", "dp"), None),
        P("seq", None, None),
        P("seq", None, None, None),
        P("seq", None, None, None),
    )
    return jax.shard_map(local, mesh=mesh, in_specs=in_specs, out_specs=out_specs, check_vma=False)
```

time: 502 us -> 221 us (0.44); the launches traced: 496 us -> 220 us
  waiting for transfers between devices: 298 us -> 65.4 us
  Pallas kernels: 0 us -> 74 us
  blocking collectives: 55.9 us -> 0 us
  matrix products: 46.3 us -> 5.51 us
  starting transfers between devices: 30.7 us -> 67.4 us
  local copies, waits for them, and re-layouts: 32 us -> 3.52 us
  other arithmetic: 18.2 us -> 3.17 us
  between operations: 14.9 us -> 0.93 us
    unnamed x3 -> x0, waiting for transfers between devices: 212 us -> none
    pallas_call x0 -> x17, Pallas kernels: none -> 74 us  [the longest x1 18.7 us: local(): call(mlp_kernel, FF // TILE, [full, full, full, full, col_blocks(1024, TI...]
    psum x1 -> x0, waiting for transfers between devices: 47.2 us -> none  [local(): lax.psum(grad_first.astype(jnp.bfloat16), 'dp').astype(jnp.float32)]
    dot_general x15 -> x1, matrix products: 46.3 us -> 5.51 us  [nn(): lax.dot_general(a, b, (((1,), (0,)), ((), ())), preferred_element_type=f32)]
    all_to_all x1 -> x0, blocking collectives: 33.8 us -> none  [local(): lax.all_to_all(cols_third, 'seq', split_axis=1, concat_axis=2, tiled=True)]
    ppermute x0 -> x15, starting transfers between devices: none -> 27.5 us  [the longest x6 10.4 us: send_around(): lax.ppermute(blocks[amount], BOTH, shift_pairs(axis, amount))]
    ppermute x0 -> x15, waiting for transfers between devices: none -> 26.8 us  [the longest x6 14.5 us: send_around(): lax.ppermute(blocks[amount], BOTH, shift_pairs(axis, amount))]
    psum x1 -> x0, blocking collectives: 22.1 us -> none  [local(): lax.psum(grad_third.astype(jnp.bfloat16), 'dp').astype(jnp.float32)]
  transfers between devices with their start and end apart: 5 -> 19, of which waited for: 4 -> 9; matrix products, arithmetic and copies ran while one was open for 11% -> 4% of each run, Pallas kernels for 0% -> 22%
where the time goes in v1:
time: 221 us; the launch traced here: 220 us
  Pallas kernels  74 us (33%)
  starting transfers between devices  67.4 us (30%)
  waiting for transfers between devices  65.4 us (30%)
  matrix products  5.51 us (2%)
  local copies, waits for them, and re-layouts  3.52 us (2%)
  other arithmetic  3.17 us (1%)
    all_to_all x4, starting transfers between devices, exchange(): return lax.all_to_all(wire, 'seq', split_axis=0, concat_axis=0, tiled=True)  39.9 us
    all_to_all x4, waiting for transfers between devices, exchange(): return lax.all_to_all(wire, 'seq', split_axis=0, concat_axis=0, tiled=True)  38.5 us
    pallas_call x1, Pallas kernels, local(): call(mlp_kernel, FF // TILE, [full, full, full, full, col_blocks(1024, TI...  18.7 us
    ppermute x6, waiting for transfers between devices, send_around(): lax.ppermute(blocks[amount], BOTH, shift_pairs(axis, amount))  14.5 us
    ppermute x6, starting transfers between devices, send_around(): lax.ppermute(blocks[amount], BOTH, shift_pairs(axis, amount))  10.4 us
    pallas_call x1, Pallas kernels, local(): call(weight_grad_kernel, FF // TILE, [place_spec, whole(D, 1024), full, v...  10.1 us
    pallas_call x1, Pallas kernels, local(): call(through_kernel, FF // TILE, [place_spec, full, row_blocks(TILE)], [c...  7.73 us
    ppermute x2, waiting for transfers between devices, sequence_sum(): return add_parts(part, lax.ppermute(part, 'dp', FAR_CHIP)).astype(bf16)  7.19 us
  transfers between devices with their start and end apart: 19, of which 9 were waited for; matrix products, arithmetic and copies ran while one was open for 4% of the time, Pallas kernels for 22%

profile of v1, /device:TPU:1, one launch (start us, length us, event | category | flops | bytes accessed | tf_op | source)
XLA Modules:
  0.0 219.9 jit_solution(4082782596193221599)
XLA Ops:
  0.7 5.0 %shard_map.162 = bf16[1024,512]{1,0:T(8,128)(2,1)} custom-call(bf16[1024,512]{1,0:T(8,128)(2,1)} %bitcast.38, f32[1,512]{1,0:T(1,128)} %bitcast.48, bf16[8,128,128]{2,1,0:T(8,128)(2,1)} %factor_ref.3), custom_call_target="tpu_custom_call" | custom-call | flops 140000000 | bytes 2400000 | tf_op jit(solution)/shard_map/pallas_call | solution.py:507
  5.7 13.5 %all-to-all-start = ((bf16[64,16,512]{2,1,0:T(8,128)(2,1)}), bf16[64,16,512]{2,1,0:T(8,128)(2,1)S(1)}, u32[]{:S(2)}, u32[]{:S(2)}) async-start(bf16[64,16,512]{2,1,0:T(8,128)(2,1)} %bitcast.53), calls=%async_computation | async-start | bytes 2097152 | tf_op jit(solution)/shard_map/all_to_all | solution.py:472
  20.2 25.1 %all-to-all-done = bf16[64,16,512]{2,1,0:T(8,128)(2,1)S(1)} async-done(((bf16[64,16,512]{2,1,0:T(8,128)(2,1)}), bf16[64,16,512]{2,1,0:T(8,128)(2,1)S(1)}, u32[]{:S(2)}, u32[]{:S(2)}) %all-to-all-start) | async-done | bytes 1048608 | tf_op jit(solution)/shard_map/all_to_all | solution.py:472
  45.3 2.4 %shard_map.164 = (bf16[1024,512]{1,0:T(8,128)(2,1)}, bf16[1024,512]{1,0:T(8,128)(2,1)}) custom-call(bf16[1024,512]{1,0:T(8,128)(2,1)S(1)} %bitcast.42, bf16[4,256,256]{2,1,0:T(8,128)(2,1)S(1)} %get-tuple-element.45.factor_ref, f32[256,16]{1,0:T(8,128)S(1)} %get-tuple-element.46.columns_ref), custom_call_target="tpu_custom_call" | custom-call | flops 280000000 | bytes 4000000 | tf_op jit(solution)/shard_map/pallas_call | solution.py:554
  47.6 8.0 %all-to-all-start.1 = ((bf16[64,16,512]{2,1,0:T(8,128)(2,1)}), bf16[64,16,512]{2,1,0:T(8,128)(2,1)S(1)}, u32[]{:S(2)}, u32[]{:S(2)}) async-start(bf16[64,16,512]{2,1,0:T(8,128)(2,1)} %bitcast.57), calls=%async_computation.1 | async-start | bytes 2097152 | tf_op jit(solution)/shard_map/all_to_all | solution.py:472
  55.6 4.1 %shard_map.165 = (bf16[1024,512]{1,0:T(8,128)(2,1)}, bf16[1024,512]{1,0:T(8,128)(2,1)}) custom-call(bf16[1024,512]{1,0:T(8,128)(2,1)} %bitcast.39, f32[1,512]{1,0:T(1,128)} %bitcast.49, f32[1,512]{1,0:T(1,128)} %bitcast.61, f32[1,512]{1,0:T(1,128)} %bitcast.63), custom_call_target="tpu_custom_call" | custom-call | flops 10000000 | bytes 4000000 | tf_op jit(solution)/shard_map/pallas_call | solution.py:531
  60.3 7.7 %shard_map.166 = (bf16[1024,2048]{1,0:T(8,128)(2,1)}, bf16[512,1024]{1,0:T(8,128)(2,1)}) custom-call(s32[4]{0:T(128)} %pad_add_fusion.place_ref, bf16[1024,512]{1,0:T(8,128)(2,1)} %bitcast.64, bf16[2048,512]{1,0:T(8,128)(2,1)} %down_ref.1), custom_call_target="tpu_custom_call" | custom-call | flops 2700000000 | bytes 14000000 | tf_op jit(solution)/shard_map/pallas_call | solution.py:542
  68.0 13.4 %all-to-all-done.1 = bf16[64,16,512]{2,1,0:T(8,128)(2,1)S(1)} async-done(((bf16[64,16,512]{2,1,0:T(8,128)(2,1)}), bf16[64,16,512]{2,1,0:T(8,128)(2,1)S(1)}, u32[]{:S(2)}, u32[]{:S(2)}) %all-to-all-start.1) | async-done | bytes 1048608 | tf_op jit(solution)/shard_map/all_to_all | solution.py:472
  82.4 18.7 %shard_map.167 = (bf16[1024,512]{1,0:T(8,128)(2,1)}, bf16[1024,2048]{1,0:T(8,128)(2,1)}, bf16[1024,2048]{1,0:T(8,128)(2,1)}, bf16[1024,512]{1,0:T(8,128)(2,1)}, bf16[1024,512]{1,0:T(8,128)(2,1)}) custom-call(bf16[1024,512]{1,0:T(8,128)(2,1)} %bitcast.40, bf16[1024,512]{1,0:T(8,128)(2,1)} %bitcast.65, bf16[1024,512]{1,0:T(8,128)(2,1)} %bitcast.51, ...), custom_call_target="tpu_custom_call" | custom-call | flops 4300000256 | bytes 20000000 | tf_op jit(solution)/shard_map/pallas_call | solution.py:568
  101.1 8.1 %all-to-all-start.2 = ((bf16[64,16,512]{2,1,0:T(8,128)(2,1)}), bf16[64,16,512]{2,1,0:T(8,128)(2,1)S(1)}, u32[]{:S(2)}, u32[]{:S(2)}) async-start(bf16[64,16,512]{2,1,0:T(8,128)(2,1)} %bitcast.56), calls=%async_computation.2 | async-start | bytes 2097152 | tf_op jit(solution)/shard_map/all_to_all | solution.py:472
  109.3 10.1 %shard_map.168 = (bf16[2,256,2048]{2,1,0:T(8,128)(2,1)}, bf16[256,2048]{1,0:T(8,128)(2,1)}, bf16[256,2048]{1,0:T(8,128)(2,1)}) custom-call(s32[4]{0:T(128)} %pad_add_fusion.place_ref, bf16[512,1024]{1,0:T(8,128)(2,1)} %get-tuple-element.53.cot_t_ref, bf16[1024,512]{1,0:T(8,128)(2,1)} %get-tuple-element.50.hidden_ref, f32[1,512]{1,0:T(1,128)} %bitcast.67, ...), custom_call_target="tpu_custom_call" | custom-call | flops 4800000000 | bytes 14000000 | tf_op jit(solution)/shard_map/pallas_call | solution.py:589
  119.3 1.9 collective-permute-start
  121.4 2.4 %collective-permute-done.up_ref = bf16[256,2048]{1,0:T(8,128)(2,1)S(1)} collective-permute-done((bf16[256,2048]{1,0:T(8,128)(2,1)}, bf16[256,2048]{1,0:T(8,128)(2,1)S(1)}, u32[]{:S(2)}, u32[]{:S(2)}) %collective-permute-start) | collective-permute-done | bytes 1048608 | tf_op jit(solution)/shard_map/ppermute | solution.py:617
  126.2 3.7 %shard_map.169 = (bf16[2,64,2048]{2,1,0:T(8,128)(2,1)}, bf16[2,64,2048]{2,1,0:T(8,128)(2,1)}, bf16[2,64,2048]{2,1,0:T(8,128)(2,1)}, bf16[2,64,2048]{2,1,0:T(8,128)(2,1)}, bf16[16,128]{1,0:T(8,128)(2,1)}) custom-call(bf16[2,256,2048]{2,1,0:T(8,128)(2,1)} %get-tuple-element.55.keep_ref, bf16[256,2048]{1,0:T(8,128)(2,1)} %copy-done.17, bf16[256,2048]{1,0:T(8,128)(2,1)} %copy-done.18), custom_call_target="tpu_custom_call" | custom-call | flops 1000 | bytes 1000 | tf_op jit(solution)/shard_map/pallas_call | solution.py:607
  131.3 2.6 %collective-permute-start.3 = (bf16[2,64,2048]{2,1,0:T(8,128)(2,1)}, bf16[2,64,2048]{2,1,0:T(8,128)(2,1)S(1)}, u32[]{:S(2)}, u32[]{:S(2)}) collective-permute-start(bf16[2,64,2048]{2,1,0:T(8,128)(2,1)} %get-tuple-element.65), channel_id=1, source_target_pairs={{0,2},{1,3},{4,6},{5,7},{2,0},{3,1},{6,4},{7,5},{8,10},{9,11},{12,... | collective-permute-start | bytes 1572872 | tf_op jit(solution)/shard_map/ppermute | solution.py:461
  135.4 3.1 %shard_map.170 = (bf16[1024,512]{1,0:T(8,128)(2,1)}, bf16[1024,512]{1,0:T(8,128)(2,1)}, bf16[16,128]{1,0:T(8,128)(2,1)}) custom-call(bf16[1024,512]{1,0:T(8,128)(2,1)S(1)} %bitcast.44, bf16[4,256,256]{2,1,0:T(8,128)(2,1)S(1)} %get-tuple-element.45.factor_ref, f32[256,16]{1,0:T(8,128)S(1)} %get-tuple-element.46.columns_ref, bf16[16,128]{1,0:T(8,128)(2,1)S(1)} %copy-done.14), custom_call_target="tpu_custom_call" | custom-call | flops 1000 | bytes 1000 | tf_op jit(solution)/shard_map/pallas_call | solution.py:620
  138.4 10.3 %all-to-all-start.3 = ((bf16[64,16,512]{2,1,0:T(8,128)(2,1)}), bf16[64,16,512]{2,1,0:T(8,128)(2,1)S(1)}, u32[]{:S(2)}, u32[]{:S(2)}) async-start(bf16[64,16,512]{2,1,0:T(8,128)(2,1)} %bitcast.37), calls=%async_computation.3 | async-start | bytes 2097152 | tf_op jit(solution)/shard_map/all_to_all | solution.py:472
  148.8 5.5 %shard_map.177 = (bf16[1056,128]{1,0:T(8,128)(2,1)}, bf16[16,128]{1,0:T(8,128)(2,1)}) custom-call(bf16[1024,512]{1,0:T(8,128)(2,1)} %bitcast.45, bf16[1024,512]{1,0:T(8,128)(2,1)} %get-tuple-element.78.second_ref, bf16[1024,512]{1,0:T(8,128)(2,1)} %bitcast.43, bf16[1024,512]{1,0:T(8,128)(2,1)} %get-tuple-element.79.back_ref), custom_call_target="tpu_custom_call" | custom-call | flops 1000 | bytes 1000 | tf_op jit(solution)/shard_map/pallas_call | solution.py:644
  155.8 9.0 %collective-permute-done.3.refs_2_ = bf16[2,64,2048]{2,1,0:T(8,128)(2,1)S(1)} collective-permute-done((bf16[2,64,2048]{2,1,0:T(8,128)(2,1)}, bf16[2,64,2048]{2,1,0:T(8,128)(2,1)S(1)}, u32[]{:S(2)}, u32[]{:S(2)}) %collective-permute-start.3) | collective-permute-done | bytes 524320 | tf_op jit(solution)/shard_map/ppermute | solution.py:461
  166.3 1.8 collective-permute-start.5
  168.1 2.1 collective-permute-start.6
  170.2 1.8 collective-permute-start.7
  172.0 2.0 collective-permute-done.5.refs_1_
  174.0 3.4 %collective-permute-done.6.refs_2_ = bf16[2,16,2048]{2,1,0:T(8,128)(2,1)S(1)} collective-permute-done((bf16[2,16,2048]{2,1,0:T(8,128)(2,1)S(1)}, bf16[2,16,2048]{2,1,0:T(8,128)(2,1)S(1)}, u32[]{:S(2)}, u32[]{:S(2)}) %collective-permute-start.6) | collective-permute-done | bytes 131104 | tf_op jit(solution)/shard_map/ppermute | solution.py:461
  177.5 3.7 %collective-permute-start.8 = (bf16[2,8,2048]{2,1,0:T(8,128)(2,1)S(1)}, bf16[2,8,2048]{2,1,0:T(8,128)(2,1)S(1)}, u32[]{:S(2)}, u32[]{:S(2)}) collective-permute-start(bf16[2,8,2048]{2,1,0:T(8,128)(2,1)S(1)} %get-tuple-element.72), channel_id=1, source_target_pairs={{0,128},{1,129},{4,132},{5,133},{2,130},{3,131},{6,134},{7,135},{8... | collective-permute-start | bytes 196616 | tf_op jit(solution)/shard_map/ppermute | solution.py:670
  181.3 1.8 collective-permute-start.14
  183.1 5.5 %add_convert_fusion.out_order_ref = bf16[1024,512]{1,0:T(8,128)(2,1)} fusion(bf16[1024,512]{1,0:T(8,128)(2,1)S(1)} %copy-done.22, bf16[1024,2048]{1,0:T(8,128)(2,1)} %get-tuple-element.51.active_ref, bf16[2048,512]{1,0:T(8,128)(2,1)S(1)} %copy-done.21), kind=kOutput, calls=%fused_computation | convolution fusion | flops 2149056512 | bytes 8388608 | tf_op jit(solution)/shard_map/dot_general | solution.py:19
  188.6 5.1 %shard_map.171 = (f32[1024,512]{1,0:T(8,128)}, bf16[16,128]{1,0:T(8,128)(2,1)}) custom-call(bf16[1024,512]{1,0:T(8,128)(2,1)} %bitcast.52, bf16[1024,512]{1,0:T(8,128)(2,1)} %get-tuple-element.48.gate_ref, f32[1,512]{1,0:T(1,128)} %bitcast.62, bf16[1024,512]{1,0:T(8,128)(2,1)} %get-tuple-element.60.grad_hidden_ref, ...), custom_call_target="tpu_custom_call" | custom-call | flops 1000000 | bytes 1000 | tf_op jit(solution)/shard_map/pallas_call | solution.py:632
  198.3 2.5 %shard_map.178 = bf16[1024,128]{1,0:T(8,128)(2,1)S(1)} custom-call(bf16[1024,512]{1,0:T(8,128)(2,1)S(1)} %bitcast.35, bf16[1024,512]{1,0:T(8,128)(2,1)S(1)} %copy-done.6, bf16[16,128]{1,0:T(8,128)(2,1)S(1)} %copy-done.12, bf16[16,128]{1,0:T(8,128)(2,1)S(1)} %copy-done.13, bf16[1024,512]{1,0:T(8,128)(2,1)S(1)} %copy-done.7), custom_call_target="tpu_custom_call" | custom-call | flops 140000000 | bytes 3000000 | tf_op jit(solution)/shard_map/pallas_call | solution.py:677
  200.8 4.7 %collective-permute-start.11 = (bf16[1024,128]{1,0:T(8,128)(2,1)S(1)}, bf16[1024,128]{1,0:T(8,128)(2,1)S(1)}, u32[]{:S(2)}, u32[]{:S(2)}) collective-permute-start(bf16[1024,128]{1,0:T(8,128)(2,1)S(1)} %shard_map.178), channel_id=1, source_target_pairs={{0,1},{1,0},{2,3},{3,2},{4,5},{5,4},{6,7},{7,6},{8,9},{9,8},{10,11... | collective-permute-start | bytes 786440 | tf_op jit(solution)/shard_map/ppermute | solution.py:467
  205.6 3.8 %shard_map.172 = bf16[1024,512]{1,0:T(8,128)(2,1)} custom-call(bf16[1024,512]{1,0:T(8,128)(2,1)S(1)} %bitcast.36, bf16[1024,512]{1,0:T(8,128)(2,1)S(1)} %bitcast.41, f32[1,512]{1,0:T(1,128)S(1)} %bitcast.50, bf16[8,128,128]{2,1,0:T(8,128)(2,1)S(1)} %copy-done.8, bf16[1024,512]{1,0:T(8,128)(2,1)S(1)} %copy-done.4, f32[1024,512]{1,0:T(8,128)S(1)} %copy-done.5), custom_call_target="tpu_custom_call" | custom-call | flops 140000000 | bytes 8000000 | tf_op jit(solution)/shard_map/pallas_call | solution.py:689
  211.8 7.2 %collective-permute-done.12 = bf16[1024,128]{1,0:T(8,128)(2,1)S(1)} collective-permute-done((bf16[1024,128]{1,0:T(8,128)(2,1)S(1)}, bf16[1024,128]{1,0:T(8,128)(2,1)S(1)}, u32[]{:S(2)}, u32[]{:S(2)}) %collective-permute-start.12) | collective-permute-done | bytes 262176 | tf_op jit(solution)/shard_map/ppermute | solution.py:468
  (83 shorter events, 18.9 us)
Async XLA Ops:
  0.6 18.5 %copy-start.20 = (bf16[2,4,4,128]{3,2,1,0:T(4,128)(2,1)S(1)}, bf16[2,4,4,128]{3,2,1,0:T(4,128)(2,1)}, u32[]{:S(2)}) copy-start(bf16[2,4,4,128]{3,2,1,0:T(4,128)(2,1)} %param.18) | copy-start | bytes 24580
  0.6 18.7 %copy-start.15 = (bf16[2,4,128,128]{3,2,1,0:T(8,128)(2,1)S(1)}, bf16[2,4,128,128]{3,2,1,0:T(8,128)(2,1)}, u32[]{:S(2)}) copy-start(bf16[2,4,128,128]{3,2,1,0:T(8,128)(2,1)} %second_ref.1) | copy-start | bytes 786436
  5.7 39.6 %all-to-all-start = ((bf16[64,16,512]{2,1,0:T(8,128)(2,1)}), bf16[64,16,512]{2,1,0:T(8,128)(2,1)S(1)}, u32[]{:S(2)}, u32[]{:S(2)}) async-start(bf16[64,16,512]{2,1,0:T(8,128)(2,1)} %bitcast.53), calls=%async_computation | async-start | bytes 2097152 | tf_op jit(solution)/shard_map/all_to_all | solution.py:472
  45.3 14.4 %copy-start.2 = (bf16[64,16,512]{2,1,0:T(8,128)(2,1)}, bf16[64,16,512]{2,1,0:T(8,128)(2,1)S(1)}, u32[]{:S(2)}) copy-start(bf16[64,16,512]{2,1,0:T(8,128)(2,1)S(1)} %all-to-all-done) | copy-start | bytes 3145732
  47.6 33.8 %all-to-all-start.1 = ((bf16[64,16,512]{2,1,0:T(8,128)(2,1)}), bf16[64,16,512]{2,1,0:T(8,128)(2,1)S(1)}, u32[]{:S(2)}, u32[]{:S(2)}) async-start(bf16[64,16,512]{2,1,0:T(8,128)(2,1)} %bitcast.57), calls=%async_computation.1 | async-start | bytes 2097152 | tf_op jit(solution)/shard_map/all_to_all | solution.py:472
  101.1 33.5 %all-to-all-start.2 = ((bf16[64,16,512]{2,1,0:T(8,128)(2,1)}), bf16[64,16,512]{2,1,0:T(8,128)(2,1)S(1)}, u32[]{:S(2)}, u32[]{:S(2)}) async-start(bf16[64,16,512]{2,1,0:T(8,128)(2,1)} %bitcast.56), calls=%async_computation.2 | async-start | bytes 2097152 | tf_op jit(solution)/shard_map/all_to_all | solution.py:472
  119.3 4.4 %collective-permute-start = (bf16[256,2048]{1,0:T(8,128)(2,1)}, bf16[256,2048]{1,0:T(8,128)(2,1)S(1)}, u32[]{:S(2)}, u32[]{:S(2)}) collective-permute-start(bf16[256,2048]{1,0:T(8,128)(2,1)} %get-tuple-element.56), channel_id=1, source_target_pairs={{0,1},{1,0},{2,3},{3,2},{4,5},{5,4},{6,7},{7,6},{8,9},{9,8},{10,11... | collective-permute-start | bytes 3145736 | tf_op jit(solution)/shard_map/ppermute | solution.py:617
  121.3 4.0 %collective-permute-start.1 = (bf16[256,2048]{1,0:T(8,128)(2,1)}, bf16[256,2048]{1,0:T(8,128)(2,1)S(1)}, u32[]{:S(2)}, u32[]{:S(2)}) collective-permute-start(bf16[256,2048]{1,0:T(8,128)(2,1)} %get-tuple-element.57), channel_id=1, source_target_pairs={{0,1},{1,0},{2,3},{3,2},{4,5},{5,4},{6,7},{7,6},{8,9},{9,8},{10,11... | collective-permute-start | bytes 3145736 | tf_op jit(solution)/shard_map/ppermute | solution.py:617
  130.0 25.8 %collective-permute-start.2 = (bf16[2,64,2048]{2,1,0:T(8,128)(2,1)}, bf16[2,64,2048]{2,1,0:T(8,128)(2,1)S(1)}, u32[]{:S(2)}, u32[]{:S(2)}) collective-permute-start(bf16[2,64,2048]{2,1,0:T(8,128)(2,1)} %get-tuple-element.64), channel_id=1, source_target_pairs={{0,4},{1,5},{4,2},{5,3},{2,6},{3,7},{6,0},{7,1},{8,12},{9,13},{12,... | collective-permute-start | bytes 1572872 | tf_op jit(solution)/shard_map/ppermute | solution.py:461
  131.3 33.5 %collective-permute-start.3 = (bf16[2,64,2048]{2,1,0:T(8,128)(2,1)}, bf16[2,64,2048]{2,1,0:T(8,128)(2,1)S(1)}, u32[]{:S(2)}, u32[]{:S(2)}) collective-permute-start(bf16[2,64,2048]{2,1,0:T(8,128)(2,1)} %get-tuple-element.65), channel_id=1, source_target_pairs={{0,2},{1,3},{4,6},{5,7},{2,0},{3,1},{6,4},{7,5},{8,10},{9,11},{12,... | collective-permute-start | bytes 1572872 | tf_op jit(solution)/shard_map/ppermute | solution.py:461
  133.9 30.9 %collective-permute-start.4 = (bf16[2,64,2048]{2,1,0:T(8,128)(2,1)}, bf16[2,64,2048]{2,1,0:T(8,128)(2,1)}, u32[]{:S(2)}, u32[]{:S(2)}) collective-permute-start(bf16[2,64,2048]{2,1,0:T(8,128)(2,1)} %get-tuple-element.66), channel_id=1, source_target_pairs={{0,6},{1,7},{4,0},{5,1},{2,4},{3,5},{6,2},{7,3},{8,14},{9,15},{12,... | collective-permute-start | bytes 1572872 | tf_op jit(solution)/shard_map/ppermute | solution.py:461
  134.7 14.1 %copy-start.3 = (bf16[64,16,512]{2,1,0:T(8,128)(2,1)}, bf16[64,16,512]{2,1,0:T(8,128)(2,1)S(1)}, u32[]{:S(2)}) copy-start(bf16[64,16,512]{2,1,0:T(8,128)(2,1)S(1)} %all-to-all-done.2) | copy-start | bytes 3145732
  138.4 59.5 %all-to-all-start.3 = ((bf16[64,16,512]{2,1,0:T(8,128)(2,1)}), bf16[64,16,512]{2,1,0:T(8,128)(2,1)S(1)}, u32[]{:S(2)}, u32[]{:S(2)}) async-start(bf16[64,16,512]{2,1,0:T(8,128)(2,1)} %bitcast.37), calls=%async_computation.3 | async-start | bytes 2097152 | tf_op jit(solution)/shard_map/all_to_all | solution.py:472
  148.8 16.0 %copy-start.9 = (bf16[2,64,2048]{2,1,0:T(8,128)(2,1)S(1)}, bf16[2,64,2048]{2,1,0:T(8,128)(2,1)}, u32[]{:S(2)}) copy-start(bf16[2,64,2048]{2,1,0:T(8,128)(2,1)} %get-tuple-element.63.refs_0_) | copy-start | bytes 1572868
  148.8 16.0 %copy-start.11 = (bf16[16,128]{1,0:T(8,128)(2,1)S(1)}, bf16[16,128]{1,0:T(8,128)(2,1)}, u32[]{:S(2)}) copy-start(bf16[16,128]{1,0:T(8,128)(2,1)} %get-tuple-element.61.order_ref.token_ref) | copy-start | bytes 12292
  154.3 23.2 %copy-start = (bf16[1024,512]{1,0:T(8,128)(2,1)S(1)}, bf16[1024,512]{1,0:T(8,128)(2,1)}, u32[]{:S(2)}) copy-start(bf16[1024,512]{1,0:T(8,128)(2,1)} %get-tuple-element.59.order_ref) | copy-start | bytes 3145732
  154.3 27.0 %copy-start.19 = (bf16[1056,128]{1,0:T(8,128)(2,1)S(1)}, bf16[1056,128]{1,0:T(8,128)(2,1)}, u32[]{:S(2)}) copy-start(bf16[1056,128]{1,0:T(8,128)(2,1)} %get-tuple-element.82) | copy-start | bytes 811012
  154.3 27.0 %collective-permute-start.13 = (bf16[1056,128]{1,0:T(8,128)(2,1)}, bf16[1056,128]{1,0:T(8,128)(2,1)S(1)}, u32[]{:S(2)}, u32[]{:S(2)}) collective-permute-start(bf16[1056,128]{1,0:T(8,128)(2,1)} %get-tuple-element.82), channel_id=1, source_target_pairs={{0,1},{1,0},{2,3},{3,2},{4,5},{5,4},{6,7},{7,6},{8,9},{9,8},{10,11... | collective-permute-start | bytes 811016 | tf_op jit(solution)/shard_map/ppermute | solution.py:467
  164.8 18.3 %copy-start.21 = (bf16[2048,512]{1,0:T(8,128)(2,1)S(1)}, bf16[2048,512]{1,0:T(8,128)(2,1)}, u32[]{:S(2)}) copy-start(bf16[2048,512]{1,0:T(8,128)(2,1)} %down_ref.1) | copy-start | bytes 6291460
  164.8 18.3 %copy-start.22 = (bf16[1024,512]{1,0:T(8,128)(2,1)S(1)}, bf16[1024,512]{1,0:T(8,128)(2,1)}, u32[]{:S(2)}) copy-start(bf16[1024,512]{1,0:T(8,128)(2,1)} %get-tuple-element.50.hidden_ref) | copy-start | bytes 3145732
  166.3 7.7 %collective-permute-start.5 = (bf16[2,16,2048]{2,1,0:T(8,128)(2,1)S(1)}, bf16[2,16,2048]{2,1,0:T(8,128)(2,1)S(1)}, u32[]{:S(2)}, u32[]{:S(2)}) collective-permute-start(bf16[2,16,2048]{2,1,0:T(8,128)(2,1)S(1)} %get-tuple-element.68), channel_id=1, source_target_pairs={{0,8},{1,9},{4,12},{5,13},{2,10},{3,11},{6,14},{7,15},{8,16},{9,17... | collective-permute-start | bytes 393224 | tf_op jit(solution)/shard_map/ppermute | solution.py:461
  168.1 9.3 %collective-permute-start.6 = (bf16[2,16,2048]{2,1,0:T(8,128)(2,1)S(1)}, bf16[2,16,2048]{2,1,0:T(8,128)(2,1)S(1)}, u32[]{:S(2)}, u32[]{:S(2)}) collective-permute-start(bf16[2,16,2048]{2,1,0:T(8,128)(2,1)S(1)} %get-tuple-element.69), channel_id=1, source_target_pairs={{0,16},{1,17},{4,20},{5,21},{2,18},{3,19},{6,22},{7,23},{8,24},{9,... | collective-permute-start | bytes 393224 | tf_op jit(solution)/shard_map/ppermute | solution.py:461
  170.2 7.2 %collective-permute-start.7 = (bf16[2,16,2048]{2,1,0:T(8,128)(2,1)S(1)}, bf16[2,16,2048]{2,1,0:T(8,128)(2,1)S(1)}, u32[]{:S(2)}, u32[]{:S(2)}) collective-permute-start(bf16[2,16,2048]{2,1,0:T(8,128)(2,1)S(1)} %get-tuple-element.70), channel_id=1, source_target_pairs={{0,24},{1,25},{4,28},{5,29},{2,26},{3,27},{6,30},{7,31},{8,0},{9,1... | collective-permute-start | bytes 393224 | tf_op jit(solution)/shard_map/ppermute | solution.py:461
  177.5 16.2 %collective-permute-start.8 = (bf16[2,8,2048]{2,1,0:T(8,128)(2,1)S(1)}, bf16[2,8,2048]{2,1,0:T(8,128)(2,1)S(1)}, u32[]{:S(2)}, u32[]{:S(2)}) collective-permute-start(bf16[2,8,2048]{2,1,0:T(8,128)(2,1)S(1)} %get-tuple-element.72), channel_id=1, source_target_pairs={{0,128},{1,129},{4,132},{5,133},{2,130},{3,131},{6,134},{7,135},{8... | collective-permute-start | bytes 196616 | tf_op jit(solution)/shard_map/ppermute | solution.py:670
  181.3 13.8 %collective-permute-start.14 = (bf16[1056,128]{1,0:T(8,128)(2,1)S(1)}, bf16[1056,128]{1,0:T(8,128)(2,1)S(1)}, u32[]{:S(2)}, u32[]{:S(2)}) collective-permute-start(bf16[1056,128]{1,0:T(8,128)(2,1)S(1)} %add_convert_fusion.2), channel_id=1, source_target_pairs={{0,2},{2,0},{1,3},{3,1},{4,6},{6,4},{5,7},{7,5},{8,10},{10,8},{9,1... | collective-permute-start | bytes 811016 | tf_op jit(solution)/shard_map/ppermute | solution.py:468
  193.8 4.1 %collective-permute-start.9 = (bf16[2,4,2048]{2,1,0:T(4,128)(2,1)S(1)}, bf16[2,4,2048]{2,1,0:T(4,128)(2,1)S(1)}, u32[]{:S(2)}, u32[]{:S(2)}) collective-permute-start(bf16[2,4,2048]{2,1,0:T(4,128)(2,1)S(1)} %get-tuple-element.74), channel_id=1, source_target_pairs={{0,64},{1,65},{4,68},{5,69},{2,66},{3,67},{6,70},{7,71},{8,72},{9,... | collective-permute-start | bytes 98312 | tf_op jit(solution)/shard_map/ppermute | solution.py:672
  197.9 7.7 %copy-start.1 = (bf16[1,1024,512]{2,1,0:T(8,128)(2,1)S(1)}, bf16[1,1024,512]{2,1,0:T(8,128)(2,1)}, u32[]{:S(2)}) copy-start(bf16[1,1024,512]{2,1,0:T(8,128)(2,1)} %param.11) | copy-start | bytes 3145732
  197.9 7.7 %copy-start.4 = (bf16[1024,512]{1,0:T(8,128)(2,1)S(1)}, bf16[1024,512]{1,0:T(8,128)(2,1)}, u32[]{:S(2)}) copy-start(bf16[1024,512]{1,0:T(8,128)(2,1)} %get-tuple-element.60.grad_hidden_ref) | copy-start | bytes 3145732
  197.9 7.7 %copy-start.5 = (f32[1024,512]{1,0:T(8,128)S(1)}, f32[1024,512]{1,0:T(8,128)}, u32[]{:S(2)}) copy-start(f32[1024,512]{1,0:T(8,128)} %get-tuple-element.62.gate_term_ref) | copy-start | bytes 6291460
  198.0 11.4 %collective-permute-start.10 = (bf16[2,2,2048]{2,1,0:T(2,128)(2,1)S(1)}, bf16[2,2,2048]{2,1,0:T(2,128)(2,1)S(1)}, u32[]{:S(2)}, u32[]{:S(2)}) collective-permute-start(bf16[2,2,2048]{2,1,0:T(2,128)(2,1)S(1)} %get-tuple-element.76), channel_id=1, source_target_pairs={{0,32},{1,33},{4,36},{5,37},{2,34},{3,35},{6,38},{7,39},{8,40},{9,... | collective-permute-start | bytes 49160 | tf_op jit(solution)/shard_map/ppermute | solution.py:674
  200.8 8.6 %collective-permute-start.11 = (bf16[1024,128]{1,0:T(8,128)(2,1)S(1)}, bf16[1024,128]{1,0:T(8,128)(2,1)S(1)}, u32[]{:S(2)}, u32[]{:S(2)}) collective-permute-start(bf16[1024,128]{1,0:T(8,128)(2,1)S(1)} %shard_map.178), channel_id=1, source_target_pairs={{0,1},{1,0},{2,3},{3,2},{4,5},{5,4},{6,7},{7,6},{8,9},{9,8},{10,11... | collective-permute-start | bytes 786440 | tf_op jit(solution)/shard_map/ppermute | solution.py:467
  209.5 9.5 %collective-permute-start.12 = (bf16[1024,128]{1,0:T(8,128)(2,1)S(1)}, bf16[1024,128]{1,0:T(8,128)(2,1)S(1)}, u32[]{:S(2)}, u32[]{:S(2)}) collective-permute-start(bf16[1024,128]{1,0:T(8,128)(2,1)S(1)} %add_convert_fusion.4), channel_id=1, source_target_pairs={{0,2},{2,0},{1,3},{3,1},{4,6},{6,4},{5,7},{7,5},{8,10},{10,8},{9,1... | collective-permute-start | bytes 786440 | tf_op jit(solution)/shard_map/ppermute | solution.py:468
  (10 other events, 37.9 us)

commit v2 on v1

--- a/solution.py
+++ b/solution.py
@@ -91,7 +91,7 @@
 
 WIDE = pltpu.VMEM((4, 1024, 128), f32)
 PAIR = 2
-PART = 256
+WIDE_TILE = 1024
 
 
 def first_kernel(tokens_ref, gain_ref, factor_ref, wire_ref, wide_ref):
@@ -141,7 +141,7 @@
 
 
 def unmix_kernel(
-    grad_ref, factor_ref, columns_ref, core_token_ref, second_ref, wire_ref, token_ref
+    grad_ref, factor_ref, columns_ref, core_token_ref, term_token_ref, second_ref, wire_ref, token_ref
 ):
     token_ref[...] = jnp.zeros_like(token_ref)
     for a in range(4):
@@ -178,42 +178,70 @@
 
 
 def mlp_kernel(
+    wire_hbm,
+    tokens_hbm,
+    gate_hbm,
+    gain_hbm,
+    up_hbm,
+    through_hbm,
+    cot_hbm,
+    hidden_hbm,
+    active_hbm,
+    grad_pre_hbm,
+    grad_hidden_hbm,
+    out_hbm,
+    wire_ref,
     tokens_ref,
+    gate_ref,
+    gain_ref,
+    up_ref,
+    through_ref,
     cot_ref,
-    wire_ref,
-    gate_ref,
-    through_ref,
-    mlp_gain_ref,
-    up_ref,
     hidden_ref,
     active_ref,
     grad_pre_ref,
     grad_hidden_ref,
-    out_ref,
     wide_ref,
     scaled_ref,
     total_ref,
+    in_sems,
+    out_sems,
 ):
-    step = pl.program_id(0)
-
-    @pl.when(step == 0)
-    def _():
-        to_wide(wide_ref, wire_ref)
-        merge = merge_digit()
-        for k in range(8):
-            rows = rows_of(k)
-            mixed = nn(merge, get_wire(wide_ref, k).astype(bf16))
-            gated = gate_ref[rows].astype(f32) * mixed
-            hidden = (tokens_ref[rows].astype(f32) + gated).astype(bf16)
-            hidden_ref[rows] = hidden
-            hidden = hidden.astype(f32)
-            scaled_ref[rows] = (hidden * inverse_of(hidden) * mlp_gain_ref[...]).astype(bf16)
-        total_ref[...] = jnp.zeros_like(total_ref)
-
-    up = up_ref[...]
-    for part in range(1024 // PART):
-        rows = rows_of(part, PART)
-        value = nn(scaled_ref[rows], up)
+    sources = (wire_hbm, tokens_hbm, gate_hbm, gain_hbm, up_hbm, through_hbm, cot_hbm)
+    targets = (wire_ref, tokens_ref, gate_ref, gain_ref, up_ref, through_ref, cot_ref)
+    fetched = [
+        pltpu.make_async_copy(source, target, in_sems.at[index])
+        for index, (source, target) in enumerate(zip(sources, targets))
+    ]
+    for copy in fetched:
+        copy.start()
+    for copy in fetched[:4]:
+        copy.wait()
+    to_wide(wide_ref, wire_ref)
+    merge, split = merge_digit(), split_digit()
+    gain = gain_ref[...]
+    stored = []
+
+    def store(source, target):
+        copy = pltpu.make_async_copy(source, target, out_sems.at[len(stored)])
+        copy.start()
+        stored.append(copy)
+
+    for k in range(8):
+        rows = rows_of(k)
+        mixed = nn(merge, get_wire(wide_ref, k).astype(bf16))
+        gated = gate_ref[rows].astype(f32) * mixed
+        hidden = (tokens_ref[rows].astype(f32) + gated).astype(bf16)
+        hidden_ref[rows] = hidden
+        hidden = hidden.astype(f32)
+        scaled_ref[rows] = (hidden * inverse_of(hidden) * gain).astype(bf16)
+    store(hidden_ref, hidden_hbm)
+    for copy in fetched[4:]:
+        copy.wait()
+    for step in range(FF // WIDE_TILE):
+        cols = slice(step * WIDE_TILE, (step + 1) * WIDE_TILE)
+        up = up_ref[:, cols]
+        value = nn(scaled_ref[...], up)
         square = value * value
         tanh = jnp.tanh(value * (GELU_SCALE + (GELU_SCALE * GELU_CUBE) * square))
         outer = 0.5 + 0.5 * tanh
@@ -221,25 +249,31 @@
         slope = outer + active * (1.0 - outer) * (
             2.0 * GELU_SCALE + (6.0 * GELU_SCALE * GELU_CUBE) * square
         )
-        active_ref[rows] = active.astype(bf16)
-        grad_pre = (through_ref[rows].astype(f32) * slope).astype(bf16)
-        grad_pre_ref[rows] = grad_pre
-        total_ref[rows] += nt(grad_pre, up)
-
-    @pl.when(step == pl.num_programs(0) - 1)
-    def _():
-        split = split_digit()
-        for k in range(8):
-            rows = rows_of(k)
-            hidden = hidden_ref[rows].astype(f32)
-            inverse = inverse_of(hidden)
-            grad_hidden = cot_ref[rows].astype(f32) + norm_back(
-                total_ref[rows], hidden * inverse, inverse, mlp_gain_ref[...]
-            )
-            grad_hidden_ref[rows] = grad_hidden.astype(bf16)
-            gated = grad_hidden * gate_ref[rows].astype(f32)
-            put_wire(wide_ref, k, nn(split, gated.astype(bf16)))
-        from_wide(out_ref, wide_ref)
+        active_ref[:, cols] = active.astype(bf16)
+        grad_pre = (through_ref[:, cols].astype(f32) * slope).astype(bf16)
+        grad_pre_ref[:, cols] = grad_pre
+        store(active_ref.at[:, cols], active_hbm.at[:, cols])
+        store(grad_pre_ref.at[:, cols], grad_pre_hbm.at[:, cols])
+        total = nt(grad_pre, up)
+        if step == 0:
+            total_ref[...] = total
+        else:
+            total_ref[...] += total
+    for k in range(8):
+        rows = rows_of(k)
+        hidden = hidden_ref[rows].astype(f32)
+        inverse = inverse_of(hidden)
+        grad_hidden = cot_ref[rows].astype(f32) + norm_back(
+            total_ref[rows], hidden * inverse, inverse, gain
+        )
+        grad_hidden_ref[rows] = grad_hidden.astype(bf16)
+        gated = grad_hidden * gate_ref[rows].astype(f32)
+        put_wire(wide_ref, k, nn(split, gated.astype(bf16)))
+    store(grad_hidden_ref, grad_hidden_hbm)
+    from_wide(wire_ref, wide_ref)
+    store(wire_ref, out_hbm)
+    for copy in stored:
+        copy.wait()
 
 
 def owner_rows(place_ref):
@@ -283,12 +317,13 @@
     for index, (left_ref, right_ref, send_ref) in enumerate(
         ((scaled_t_ref, grad_pre_ref, send_up_ref), (cot_t_ref, active_ref, send_down_ref))
     ):
-        keep_ref[index] = nn(left_ref[0:256], right_ref[...]).astype(bf16)
-        send_ref[...] = nn(left_ref[256:512], right_ref[...]).astype(bf16)
+        product = nn(left_ref[...], right_ref[...]).astype(bf16)
+        keep_ref[index] = product[0:256]
+        send_ref[...] = product[256:512]
 
 
 def gate_term_kernel(
-    wire_ref, gate_ref, gate_weight_ref, grad_hidden_ref, order_ref, term_ref, token_ref, wide_ref
+    wire_ref, gate_ref, gate_weight_ref, grad_hidden_ref, term_ref, token_ref, wide_ref
 ):
     step = pl.program_id(0)
 
@@ -307,7 +342,7 @@
 
 
 def first_grad_kernel(
-    wire_ref, input_ref, factor_order_ref, term_order_ref, out_order_ref, out_ref, wide_ref
+    wire_ref, input_ref, factor_order_ref, out_order_ref, out_ref, wide_ref
 ):
     step = pl.program_id(0)
 
@@ -502,6 +537,7 @@
     steps = 8 // PAIR
     wide_columns = shape((1024, FF), bf16)
     held16, held_token = held((1024, D), bf16), held((16, 128), bf16)
+    held_wide = held((1024, FF), bf16)
     token_spec, token_shape = whole(16, 128), shape((16, 128), bf16)
 
     wire = call(
@@ -565,25 +601,36 @@
     wire = exchange(wire)
 
     mixed_wire = wire
+    pinned = pl.BlockSpec(memory_space=pltpu.HBM)
+    room16, room_wide = pltpu.VMEM((1024, D), bf16), pltpu.VMEM((1024, FF), bf16)
     hidden, active, grad_pre, grad_hidden, wire = call(
         mlp_kernel,
-        FF // TILE,
+        1,
+        [pl.BlockSpec(memory_space=pl.ANY)] + [pinned] * 6,
+        [pinned] * 5,
+        [held16, held_wide, held_wide, held16, held16],
         [
-            full,
-            full,
-            full,
-            full,
-            col_blocks(1024, TILE),
-            vector,
-            col_blocks(D, TILE),
+            room16,
+            room16,
+            room16,
+            pltpu.VMEM((1, D), f32),
+            pltpu.VMEM((D, FF), bf16),
+            room_wide,
+            room16,
+            room16,
+            room_wide,
+            room_wide,
+            room16,
+            WIDE,
+            room16,
+            pltpu.VMEM((1024, D), f32),
+            pltpu.SemaphoreType.DMA((7,)),
+            pltpu.SemaphoreType.DMA((3 + 2 * (FF // WIDE_TILE),)),
         ],
-        [full, col_blocks(1024, TILE), col_blocks(1024, TILE), full, full],
-        [rows16, wide_columns, wide_columns, rows16, rows16],
-        [WIDE, pltpu.VMEM((1024, D), bf16), pltpu.VMEM((1024, D), f32)],
         4_300_000_000,
         20_000_000,
         56,
-    )(tokens, cot, wire, gate, through, mlp_gain, up_weight)
+    )(wire, tokens, gate, mlp_gain, up_weight, through, cot)
     grad_mixed = exchange(wire)
 
     keep, send_up, send_down = call(
@@ -604,6 +651,17 @@
         14_000_000,
         56,
     )(place, cot_t, hidden, mlp_gain, active, grad_pre)
+    gate_term, term_token = call(
+        gate_term_kernel,
+        steps,
+        [full, pair_rows, vector, pair_rows],
+        [pair_rows, token_spec],
+        [rows32, token_shape],
+        [WIDE],
+        1_000_000,
+        1_000,
+        56,
+    )(mixed_wire, gate, gate_weight, grad_hidden)
     *blocks, core_token = call(
         core_sum_kernel,
         1,
@@ -620,26 +678,15 @@
     back_second, wire, token = call(
         unmix_kernel,
         2,
-        [col_blocks(1024, 256), whole(4, 256, 256), whole(256, 16), token_spec],
+        [col_blocks(1024, 256), whole(4, 256, 256), whole(256, 16), token_spec, token_spec],
         [col_blocks(1024, 256), col_blocks(1024, 256), token_spec],
         [held16, held16, held_token],
         [],
         1_000,
         1_000,
         24,
-    )(grad_mixed, wide_factor, columns, core_token)
+    )(grad_mixed, wide_factor, columns, core_token, term_token)
     back = exchange(wire)
-    gate_term, term_token = call(
-        gate_term_kernel,
-        steps,
-        [full, pair_rows, vector, pair_rows, token_spec],
-        [pair_rows, token_spec],
-        [rows32, token_shape],
-        [WIDE],
-        1_000_000,
-        1_000,
-        56,
-    )(mixed_wire, gate, gate_weight, grad_hidden, token)
     block_out = (hidden.astype(f32) + nn(active, down_weight)).astype(bf16)
     factor_grads, factor_token = call(
         factor_grad_kernel,
@@ -677,14 +724,14 @@
     grad_first = call(
         first_grad_kernel,
         steps,
-        [full, pair_rows, token_spec, token_spec, pl.BlockSpec(memory_space=pl.ANY)],
+        [full, pair_rows, token_spec, pl.BlockSpec(memory_space=pl.ANY)],
         row_blocks(PAIR * 128, 128),
         shape((1024, 128), bf16),
         [WIDE],
         140_000_000,
         3_000_000,
         24,
-    )(back, mixer_in, factor_token, term_token, block_out)
+    )(back, mixer_in, factor_token, block_out)
     grad_first = sequence_sum(grad_first)
     grad_tokens = call(
         token_grad_kernel,

time: 221 us -> 215 us (0.973); the launches traced: 220 us -> 211 us
  waiting for transfers between devices: 65.4 us -> 60.8 us
  Pallas kernels: 74 us -> 69.6 us
    ppermute x6, waiting for transfers between devices: 14.5 us -> 9.19 us  [send_around(): lax.ppermute(blocks[amount], BOTH, shift_pairs(axis, amount))]
    pallas_call x3, Pallas kernels: 26.3 us -> 21.6 us  [the longest x1 14.1 us: local(): call(mlp_kernel, 1, [pl.BlockSpec(memory_space=pl.ANY)] + [pinned] * 6, [...]
  transfers between devices with their start and end apart: 19 -> 19, of which waited for: 9 -> 10; matrix products, arithmetic and copies ran while one was open for 4% -> 4% of each run, Pallas kernels for 22% -> 23%
where the time goes in v2:
time: 215 us; the launch traced here: 211 us
  Pallas kernels  69.6 us (32%)
  starting transfers between devices  66.8 us (31%)
  waiting for transfers between devices  60.8 us (28%)
  matrix products  5.49 us (3%)
  local copies, waits for them, and re-layouts  3.52 us (2%)
  other arithmetic  3.17 us (1%)
    all_to_all x4, starting transfers between devices, exchange(): return lax.all_to_all(wire, 'seq', split_axis=0, concat_axis=0, tiled=True)  40.1 us
    all_to_all x4, waiting for transfers between devices, exchange(): return lax.all_to_all(wire, 'seq', split_axis=0, concat_axis=0, tiled=True)  38.5 us
    pallas_call x1, Pallas kernels, local(): call(mlp_kernel, 1, [pl.BlockSpec(memory_space=pl.ANY)] + [pinned] * 6, [...  14.1 us
    ppermute x6, starting transfers between devices, send_around(): lax.ppermute(blocks[amount], BOTH, shift_pairs(axis, amount))  10.5 us
    pallas_call x1, Pallas kernels, local(): call(weight_grad_kernel, FF // TILE, [place_spec, whole(D, 1024), full, v...  10.4 us
    ppermute x6, waiting for transfers between devices, send_around(): lax.ppermute(blocks[amount], BOTH, shift_pairs(axis, amount))  9.19 us
    pallas_call x1, Pallas kernels, local(): call(through_kernel, FF // TILE, [place_spec, full, row_blocks(TILE)], [c...  7.73 us
    ppermute x2, waiting for transfers between devices, sequence_sum(): return add_parts(part, lax.ppermute(part, 'dp', FAR_CHIP)).astype(bf16)  7.62 us
  transfers between devices with their start and end apart: 19, of which 10 were waited for; matrix products, arithmetic and copies ran while one was open for 4% of the time, Pallas kernels for 23%

profile of v2, /device:TPU:1, one launch (start us, length us, event | category | flops | bytes accessed | tf_op | source)
XLA Modules:
  0.0 210.8 jit_solution(4396651222022168856)
XLA Ops:
  0.7 5.0 %shard_map.162 = bf16[1024,512]{1,0:T(8,128)(2,1)} custom-call(bf16[1024,512]{1,0:T(8,128)(2,1)} %bitcast.38, f32[1,512]{1,0:T(1,128)} %bitcast.48, bf16[8,128,128]{2,1,0:T(8,128)(2,1)} %factor_ref.3), custom_call_target="tpu_custom_call" | custom-call | flops 140000000 | bytes 2400000 | tf_op jit(solution)/shard_map/pallas_call | solution.py:543
  5.7 13.5 %all-to-all-start = ((bf16[64,16,512]{2,1,0:T(8,128)(2,1)}), bf16[64,16,512]{2,1,0:T(8,128)(2,1)S(1)}, u32[]{:S(2)}, u32[]{:S(2)}) async-start(bf16[64,16,512]{2,1,0:T(8,128)(2,1)} %bitcast.51), calls=%async_computation | async-start | bytes 2097152 | tf_op jit(solution)/shard_map/all_to_all | solution.py:507
  20.2 25.1 %all-to-all-done = bf16[64,16,512]{2,1,0:T(8,128)(2,1)S(1)} async-done(((bf16[64,16,512]{2,1,0:T(8,128)(2,1)}), bf16[64,16,512]{2,1,0:T(8,128)(2,1)S(1)}, u32[]{:S(2)}, u32[]{:S(2)}) %all-to-all-start) | async-done | bytes 1048608 | tf_op jit(solution)/shard_map/all_to_all | solution.py:507
  45.3 2.4 %shard_map.164 = (bf16[1024,512]{1,0:T(8,128)(2,1)}, bf16[1024,512]{1,0:T(8,128)(2,1)}) custom-call(bf16[1024,512]{1,0:T(8,128)(2,1)S(1)} %bitcast.42, bf16[4,256,256]{2,1,0:T(8,128)(2,1)S(1)} %get-tuple-element.45.factor_ref, f32[256,16]{1,0:T(8,128)S(1)} %get-tuple-element.46.columns_ref), custom_call_target="tpu_custom_call" | custom-call | flops 280000000 | bytes 4000000 | tf_op jit(solution)/shard_map/pallas_call | solution.py:590
  47.6 8.1 %all-to-all-start.1 = ((bf16[64,16,512]{2,1,0:T(8,128)(2,1)}), bf16[64,16,512]{2,1,0:T(8,128)(2,1)S(1)}, u32[]{:S(2)}, u32[]{:S(2)}) async-start(bf16[64,16,512]{2,1,0:T(8,128)(2,1)} %bitcast.57), calls=%async_computation.1 | async-start | bytes 2097152 | tf_op jit(solution)/shard_map/all_to_all | solution.py:507
  55.8 4.1 %shard_map.165 = (bf16[1024,512]{1,0:T(8,128)(2,1)}, bf16[1024,512]{1,0:T(8,128)(2,1)}) custom-call(bf16[1024,512]{1,0:T(8,128)(2,1)} %bitcast.39, f32[1,512]{1,0:T(1,128)} %bitcast.49, f32[1,512]{1,0:T(1,128)} %bitcast.61, f32[1,512]{1,0:T(1,128)} %bitcast.63), custom_call_target="tpu_custom_call" | custom-call | flops 10000000 | bytes 4000000 | tf_op jit(solution)/shard_map/pallas_call | solution.py:567
  60.4 7.7 %shard_map.166 = (bf16[1024,2048]{1,0:T(8,128)(2,1)}, bf16[512,1024]{1,0:T(8,128)(2,1)}) custom-call(s32[4]{0:T(128)} %pad_add_fusion.place_ref, bf16[1024,512]{1,0:T(8,128)(2,1)} %bitcast.64, bf16[2048,512]{1,0:T(8,128)(2,1)} %down_ref.1), custom_call_target="tpu_custom_call" | custom-call | flops 2700000000 | bytes 14000000 | tf_op jit(solution)/shard_map/pallas_call | solution.py:578
  68.2 13.4 %all-to-all-done.1 = bf16[64,16,512]{2,1,0:T(8,128)(2,1)S(1)} async-done(((bf16[64,16,512]{2,1,0:T(8,128)(2,1)}), bf16[64,16,512]{2,1,0:T(8,128)(2,1)S(1)}, u32[]{:S(2)}, u32[]{:S(2)}) %all-to-all-start.1) | async-done | bytes 1048608 | tf_op jit(solution)/shard_map/all_to_all | solution.py:507
  82.6 14.1 %shard_map.167 = (bf16[1024,512]{1,0:T(8,128)(2,1)}, bf16[1024,2048]{1,0:T(8,128)(2,1)}, bf16[1024,2048]{1,0:T(8,128)(2,1)}, bf16[1024,512]{1,0:T(8,128)(2,1)}, bf16[1024,512]{1,0:T(8,128)(2,1)}) custom-call(bf16[1024,512]{1,0:T(8,128)(2,1)} %bitcast.52, bf16[1024,512]{1,0:T(8,128)(2,1)} %bitcast.40, bf16[1024,512]{1,0:T(8,128)(2,1)} %get-tuple-element.48.gate_hbm.gate_ref, ...), custom_call_target="tpu_custom_call" | custom-call | flops 4300000256 | bytes 20000000 | tf_op jit(solution)/shard_map/pallas_call | solution.py:606
  96.6 8.1 %all-to-all-start.2 = ((bf16[64,16,512]{2,1,0:T(8,128)(2,1)}), bf16[64,16,512]{2,1,0:T(8,128)(2,1)S(1)}, u32[]{:S(2)}, u32[]{:S(2)}) async-start(bf16[64,16,512]{2,1,0:T(8,128)(2,1)} %bitcast.56), calls=%async_computation.2 | async-start | bytes 2097152 | tf_op jit(solution)/shard_map/all_to_all | solution.py:507
  104.8 10.4 %shard_map.168 = (bf16[2,256,2048]{2,1,0:T(8,128)(2,1)}, bf16[256,2048]{1,0:T(8,128)(2,1)}, bf16[256,2048]{1,0:T(8,128)(2,1)}) custom-call(s32[4]{0:T(128)} %pad_add_fusion.place_ref, bf16[512,1024]{1,0:T(8,128)(2,1)} %get-tuple-element.53.cot_t_ref, bf16[1024,512]{1,0:T(8,128)(2,1)} %get-tuple-element.50.hidden_ref, f32[1,512]{1,0:T(1,128)} %bitcast.67, ...), custom_call_target="tpu_custom_call" | custom-call | flops 4800000000 | bytes 14000000 | tf_op jit(solution)/shard_map/pallas_call | solution.py:636
  115.2 1.9 collective-permute-start
  117.2 2.4 %collective-permute-done.up_ref = bf16[256,2048]{1,0:T(8,128)(2,1)S(1)} collective-permute-done((bf16[256,2048]{1,0:T(8,128)(2,1)}, bf16[256,2048]{1,0:T(8,128)(2,1)S(1)}, u32[]{:S(2)}, u32[]{:S(2)}) %collective-permute-start) | collective-permute-done | bytes 1048608 | tf_op jit(solution)/shard_map/ppermute | solution.py:675
  122.1 3.7 %shard_map.169 = (bf16[2,64,2048]{2,1,0:T(8,128)(2,1)}, bf16[2,64,2048]{2,1,0:T(8,128)(2,1)}, bf16[2,64,2048]{2,1,0:T(8,128)(2,1)}, bf16[2,64,2048]{2,1,0:T(8,128)(2,1)}, bf16[16,128]{1,0:T(8,128)(2,1)}) custom-call(bf16[2,256,2048]{2,1,0:T(8,128)(2,1)} %get-tuple-element.55.keep_ref, bf16[256,2048]{1,0:T(8,128)(2,1)} %copy-done.17, bf16[256,2048]{1,0:T(8,128)(2,1)} %copy-done.18), custom_call_target="tpu_custom_call" | custom-call | flops 1000 | bytes 1000 | tf_op jit(solution)/shard_map/pallas_call | solution.py:665
  127.0 2.6 %collective-permute-start.3 = (bf16[2,64,2048]{2,1,0:T(8,128)(2,1)}, bf16[2,64,2048]{2,1,0:T(8,128)(2,1)S(1)}, u32[]{:S(2)}, u32[]{:S(2)}) collective-permute-start(bf16[2,64,2048]{2,1,0:T(8,128)(2,1)} %get-tuple-element.66), channel_id=1, source_target_pairs={{0,2},{1,3},{4,6},{5,7},{2,0},{3,1},{6,4},{7,5},{8,10},{9,11},{12,... | collective-permute-start | bytes 1572872 | tf_op jit(solution)/shard_map/ppermute | solution.py:496
  130.4 5.1 %shard_map.170 = (f32[1024,512]{1,0:T(8,128)}, bf16[16,128]{1,0:T(8,128)(2,1)}) custom-call(bf16[1024,512]{1,0:T(8,128)(2,1)} %bitcast.53, bf16[1024,512]{1,0:T(8,128)(2,1)} %get-tuple-element.48.gate_hbm.gate_ref, f32[1,512]{1,0:T(1,128)} %bitcast.62, bf16[1024,512]{1,0:T(8,128)(2,1)} %get-tuple-element.59.grad_hidden_ref), custom_call_target="tpu_custom_call" | custom-call | flops 1000000 | bytes 1000 | tf_op jit(solution)/shard_map/pallas_call | solution.py:654
  136.2 3.1 %shard_map.171 = (bf16[1024,512]{1,0:T(8,128)(2,1)}, bf16[1024,512]{1,0:T(8,128)(2,1)}, bf16[16,128]{1,0:T(8,128)(2,1)}) custom-call(bf16[1024,512]{1,0:T(8,128)(2,1)S(1)} %bitcast.44, bf16[4,256,256]{2,1,0:T(8,128)(2,1)S(1)} %get-tuple-element.45.factor_ref, f32[256,16]{1,0:T(8,128)S(1)} %get-tuple-element.46.columns_ref, bf16[16,128]{1,0:T(8,128)(2,1)S(1)} %copy-done.13, ...), custom_call_target="tpu_custom_call" | custom-call | flops 1000 | bytes 1000 | tf_op jit(solution)/shard_map/pallas_call | solution.py:678
  139.3 10.3 %all-to-all-start.3 = ((bf16[64,16,512]{2,1,0:T(8,128)(2,1)}), bf16[64,16,512]{2,1,0:T(8,128)(2,1)S(1)}, u32[]{:S(2)}, u32[]{:S(2)}) async-start(bf16[64,16,512]{2,1,0:T(8,128)(2,1)} %bitcast.37), calls=%async_computation.3 | async-start | bytes 2097152 | tf_op jit(solution)/shard_map/all_to_all | solution.py:507
  149.7 5.5 %shard_map.177 = (bf16[1056,128]{1,0:T(8,128)(2,1)}, bf16[16,128]{1,0:T(8,128)(2,1)}) custom-call(bf16[1024,512]{1,0:T(8,128)(2,1)} %bitcast.45, bf16[1024,512]{1,0:T(8,128)(2,1)} %get-tuple-element.79.second_ref, bf16[1024,512]{1,0:T(8,128)(2,1)} %bitcast.43, bf16[1024,512]{1,0:T(8,128)(2,1)} %get-tuple-element.80.back_ref), custom_call_target="tpu_custom_call" | custom-call | flops 1000 | bytes 1000 | tf_op jit(solution)/shard_map/pallas_call | solution.py:691
  158.4 1.6 collective-permute-start.5
  160.0 2.2 %collective-permute-start.6 = (bf16[2,16,2048]{2,1,0:T(8,128)(2,1)S(1)}, bf16[2,16,2048]{2,1,0:T(8,128)(2,1)S(1)}, u32[]{:S(2)}, u32[]{:S(2)}) collective-permute-start(bf16[2,16,2048]{2,1,0:T(8,128)(2,1)S(1)} %get-tuple-element.70), channel_id=1, source_target_pairs={{0,16},{1,17},{4,20},{5,21},{2,18},{3,19},{6,22},{7,23},{8,24},{9,... | collective-permute-start | bytes 393224 | tf_op jit(solution)/shard_map/ppermute | solution.py:496
  162.2 2.0 collective-permute-start.7
  164.2 2.9 %collective-permute-done.5.refs_1_ = bf16[2,16,2048]{2,1,0:T(8,128)(2,1)S(1)} collective-permute-done((bf16[2,16,2048]{2,1,0:T(8,128)(2,1)S(1)}, bf16[2,16,2048]{2,1,0:T(8,128)(2,1)S(1)}, u32[]{:S(2)}, u32[]{:S(2)}) %collective-permute-start.5) | collective-permute-done | bytes 131104 | tf_op jit(solution)/shard_map/ppermute | solution.py:496
  167.1 6.1 %collective-permute-done.6.refs_2_ = bf16[2,16,2048]{2,1,0:T(8,128)(2,1)S(1)} collective-permute-done((bf16[2,16,2048]{2,1,0:T(8,128)(2,1)S(1)}, bf16[2,16,2048]{2,1,0:T(8,128)(2,1)S(1)}, u32[]{:S(2)}, u32[]{:S(2)}) %collective-permute-start.6) | collective-permute-done | bytes 131104 | tf_op jit(solution)/shard_map/ppermute | solution.py:496
  173.2 3.8 %collective-permute-start.8 = (bf16[2,8,2048]{2,1,0:T(8,128)(2,1)S(1)}, bf16[2,8,2048]{2,1,0:T(8,128)(2,1)S(1)}, u32[]{:S(2)}, u32[]{:S(2)}) collective-permute-start(bf16[2,8,2048]{2,1,0:T(8,128)(2,1)S(1)} %get-tuple-element.73), channel_id=1, source_target_pairs={{0,128},{1,129},{4,132},{5,133},{2,130},{3,131},{6,134},{7,135},{8... | collective-permute-start | bytes 196616 | tf_op jit(solution)/shard_map/ppermute | solution.py:717
  178.5 5.5 %add_convert_fusion.out_order_ref = bf16[1024,512]{1,0:T(8,128)(2,1)} fusion(bf16[1024,512]{1,0:T(8,128)(2,1)S(1)} %copy-done.22, bf16[1024,2048]{1,0:T(8,128)(2,1)} %get-tuple-element.51.active_ref, bf16[2048,512]{1,0:T(8,128)(2,1)S(1)} %copy-done.21), kind=kOutput, calls=%fused_computation | convolution fusion | flops 2149056512 | bytes 8388608 | tf_op jit(solution)/shard_map/dot_general | solution.py:19
  186.2 1.6 collective-permute-done.9.refs_1_
  189.3 2.5 %shard_map.178 = bf16[1024,128]{1,0:T(8,128)(2,1)S(1)} custom-call(bf16[1024,512]{1,0:T(8,128)(2,1)S(1)} %bitcast.35, bf16[1024,512]{1,0:T(8,128)(2,1)S(1)} %copy-done.6, bf16[16,128]{1,0:T(8,128)(2,1)S(1)} %copy-done.11, bf16[1024,512]{1,0:T(8,128)(2,1)S(1)} %copy-done.7), custom_call_target="tpu_custom_call" | custom-call | flops 140000000 | bytes 3000000 | tf_op jit(solution)/shard_map/pallas_call | solution.py:724
  191.8 4.2 %collective-permute-start.11 = (bf16[1024,128]{1,0:T(8,128)(2,1)S(1)}, bf16[1024,128]{1,0:T(8,128)(2,1)S(1)}, u32[]{:S(2)}, u32[]{:S(2)}) collective-permute-start(bf16[1024,128]{1,0:T(8,128)(2,1)S(1)} %shard_map.178), channel_id=1, source_target_pairs={{0,1},{1,0},{2,3},{3,2},{4,5},{5,4},{6,7},{7,6},{8,9},{9,8},{10,11... | collective-permute-start | bytes 786440 | tf_op jit(solution)/shard_map/ppermute | solution.py:502
  196.0 3.8 %shard_map.172 = bf16[1024,512]{1,0:T(8,128)(2,1)} custom-call(bf16[1024,512]{1,0:T(8,128)(2,1)S(1)} %bitcast.36, bf16[1024,512]{1,0:T(8,128)(2,1)S(1)} %bitcast.41, f32[1,512]{1,0:T(1,128)S(1)} %bitcast.50, bf16[8,128,128]{2,1,0:T(8,128)(2,1)S(1)} %copy-done.8, bf16[1024,512]{1,0:T(8,128)(2,1)S(1)} %copy-done.4, f32[1024,512]{1,0:T(8,128)S(1)} %copy-done.5), custom_call_target="tpu_custom_call" | custom-call | flops 140000000 | bytes 8000000 | tf_op jit(solution)/shard_map/pallas_call | solution.py:736
  199.9 1.6 collective-permute-start.12
  202.1 7.3 %collective-permute-done.12 = bf16[1024,128]{1,0:T(8,128)(2,1)S(1)} collective-permute-done((bf16[1024,128]{1,0:T(8,128)(2,1)S(1)}, bf16[1024,128]{1,0:T(8,128)(2,1)S(1)}, u32[]{:S(2)}, u32[]{:S(2)}) %collective-permute-start.12) | collective-permute-done | bytes 262176 | tf_op jit(solution)/shard_map/ppermute | solution.py:503
  (83 shorter events, 17.8 us)
Async XLA Ops:
  0.6 18.5 %copy-start.20 = (bf16[2,4,4,128]{3,2,1,0:T(4,128)(2,1)S(1)}, bf16[2,4,4,128]{3,2,1,0:T(4,128)(2,1)}, u32[]{:S(2)}) copy-start(bf16[2,4,4,128]{3,2,1,0:T(4,128)(2,1)} %param.18) | copy-start | bytes 24580
  0.6 18.7 %copy-start.15 = (bf16[2,4,128,128]{3,2,1,0:T(8,128)(2,1)S(1)}, bf16[2,4,128,128]{3,2,1,0:T(8,128)(2,1)}, u32[]{:S(2)}) copy-start(bf16[2,4,128,128]{3,2,1,0:T(8,128)(2,1)} %second_ref.1) | copy-start | bytes 786436
  5.7 39.6 %all-to-all-start = ((bf16[64,16,512]{2,1,0:T(8,128)(2,1)}), bf16[64,16,512]{2,1,0:T(8,128)(2,1)S(1)}, u32[]{:S(2)}, u32[]{:S(2)}) async-start(bf16[64,16,512]{2,1,0:T(8,128)(2,1)} %bitcast.51), calls=%async_computation | async-start | bytes 2097152 | tf_op jit(solution)/shard_map/all_to_all | solution.py:507
  45.3 14.6 %copy-start.2 = (bf16[64,16,512]{2,1,0:T(8,128)(2,1)}, bf16[64,16,512]{2,1,0:T(8,128)(2,1)S(1)}, u32[]{:S(2)}) copy-start(bf16[64,16,512]{2,1,0:T(8,128)(2,1)S(1)} %all-to-all-done) | copy-start | bytes 3145732
  47.6 34.0 %all-to-all-start.1 = ((bf16[64,16,512]{2,1,0:T(8,128)(2,1)}), bf16[64,16,512]{2,1,0:T(8,128)(2,1)S(1)}, u32[]{:S(2)}, u32[]{:S(2)}) async-start(bf16[64,16,512]{2,1,0:T(8,128)(2,1)} %bitcast.57), calls=%async_computation.1 | async-start | bytes 2097152 | tf_op jit(solution)/shard_map/all_to_all | solution.py:507
  96.6 38.9 %all-to-all-start.2 = ((bf16[64,16,512]{2,1,0:T(8,128)(2,1)}), bf16[64,16,512]{2,1,0:T(8,128)(2,1)S(1)}, u32[]{:S(2)}, u32[]{:S(2)}) async-start(bf16[64,16,512]{2,1,0:T(8,128)(2,1)} %bitcast.56), calls=%async_computation.2 | async-start | bytes 2097152 | tf_op jit(solution)/shard_map/all_to_all | solution.py:507
  115.2 4.4 %collective-permute-start = (bf16[256,2048]{1,0:T(8,128)(2,1)}, bf16[256,2048]{1,0:T(8,128)(2,1)S(1)}, u32[]{:S(2)}, u32[]{:S(2)}) collective-permute-start(bf16[256,2048]{1,0:T(8,128)(2,1)} %get-tuple-element.56), channel_id=1, source_target_pairs={{0,1},{1,0},{2,3},{3,2},{4,5},{5,4},{6,7},{7,6},{8,9},{9,8},{10,11... | collective-permute-start | bytes 3145736 | tf_op jit(solution)/shard_map/ppermute | solution.py:675
  117.1 4.0 %collective-permute-start.1 = (bf16[256,2048]{1,0:T(8,128)(2,1)}, bf16[256,2048]{1,0:T(8,128)(2,1)S(1)}, u32[]{:S(2)}, u32[]{:S(2)}) collective-permute-start(bf16[256,2048]{1,0:T(8,128)(2,1)} %get-tuple-element.57), channel_id=1, source_target_pairs={{0,1},{1,0},{2,3},{3,2},{4,5},{5,4},{6,7},{7,6},{8,9},{9,8},{10,11... | collective-permute-start | bytes 3145736 | tf_op jit(solution)/shard_map/ppermute | solution.py:675
  125.7 9.8 %copy-start.13 = (bf16[16,128]{1,0:T(8,128)(2,1)S(1)}, bf16[16,128]{1,0:T(8,128)(2,1)}, u32[]{:S(2)}) copy-start(bf16[16,128]{1,0:T(8,128)(2,1)} %get-tuple-element.58.core_token_ref) | copy-start | bytes 12292
  125.7 30.9 %collective-permute-start.2 = (bf16[2,64,2048]{2,1,0:T(8,128)(2,1)}, bf16[2,64,2048]{2,1,0:T(8,128)(2,1)S(1)}, u32[]{:S(2)}, u32[]{:S(2)}) collective-permute-start(bf16[2,64,2048]{2,1,0:T(8,128)(2,1)} %get-tuple-element.65), channel_id=1, source_target_pairs={{0,4},{1,5},{4,2},{5,3},{2,6},{3,7},{6,0},{7,1},{8,12},{9,13},{12,... | collective-permute-start | bytes 1572872 | tf_op jit(solution)/shard_map/ppermute | solution.py:496
  127.0 29.9 %collective-permute-start.3 = (bf16[2,64,2048]{2,1,0:T(8,128)(2,1)}, bf16[2,64,2048]{2,1,0:T(8,128)(2,1)S(1)}, u32[]{:S(2)}, u32[]{:S(2)}) collective-permute-start(bf16[2,64,2048]{2,1,0:T(8,128)(2,1)} %get-tuple-element.66), channel_id=1, source_target_pairs={{0,2},{1,3},{4,6},{5,7},{2,0},{3,1},{6,4},{7,5},{8,10},{9,11},{12,... | collective-permute-start | bytes 1572872 | tf_op jit(solution)/shard_map/ppermute | solution.py:496
  129.6 27.2 %collective-permute-start.4 = (bf16[2,64,2048]{2,1,0:T(8,128)(2,1)}, bf16[2,64,2048]{2,1,0:T(8,128)(2,1)}, u32[]{:S(2)}, u32[]{:S(2)}) collective-permute-start(bf16[2,64,2048]{2,1,0:T(8,128)(2,1)} %get-tuple-element.67), channel_id=1, source_target_pairs={{0,6},{1,7},{4,0},{5,1},{2,4},{3,5},{6,2},{7,3},{8,14},{9,15},{12,... | collective-permute-start | bytes 1572872 | tf_op jit(solution)/shard_map/ppermute | solution.py:496
  135.5 14.2 %copy-start.3 = (bf16[64,16,512]{2,1,0:T(8,128)(2,1)}, bf16[64,16,512]{2,1,0:T(8,128)(2,1)S(1)}, u32[]{:S(2)}) copy-start(bf16[64,16,512]{2,1,0:T(8,128)(2,1)S(1)} %all-to-all-done.2) | copy-start | bytes 3145732
  139.3 48.5 %all-to-all-start.3 = ((bf16[64,16,512]{2,1,0:T(8,128)(2,1)}), bf16[64,16,512]{2,1,0:T(8,128)(2,1)S(1)}, u32[]{:S(2)}, u32[]{:S(2)}) async-start(bf16[64,16,512]{2,1,0:T(8,128)(2,1)} %bitcast.37), calls=%async_computation.3 | async-start | bytes 2097152 | tf_op jit(solution)/shard_map/all_to_all | solution.py:507
  155.2 18.0 %copy-start = (bf16[1024,512]{1,0:T(8,128)(2,1)S(1)}, bf16[1024,512]{1,0:T(8,128)(2,1)}, u32[]{:S(2)}) copy-start(bf16[1024,512]{1,0:T(8,128)(2,1)} %get-tuple-element.61.order_ref) | copy-start | bytes 3145732
  155.2 21.9 %copy-start.19 = (bf16[1056,128]{1,0:T(8,128)(2,1)S(1)}, bf16[1056,128]{1,0:T(8,128)(2,1)}, u32[]{:S(2)}) copy-start(bf16[1056,128]{1,0:T(8,128)(2,1)} %get-tuple-element.82) | copy-start | bytes 811012
  155.2 21.9 %collective-permute-start.13 = (bf16[1056,128]{1,0:T(8,128)(2,1)}, bf16[1056,128]{1,0:T(8,128)(2,1)S(1)}, u32[]{:S(2)}, u32[]{:S(2)}) collective-permute-start(bf16[1056,128]{1,0:T(8,128)(2,1)} %get-tuple-element.82), channel_id=1, source_target_pairs={{0,1},{1,0},{2,3},{3,2},{4,5},{5,4},{6,7},{7,6},{8,9},{9,8},{10,11... | collective-permute-start | bytes 811016 | tf_op jit(solution)/shard_map/ppermute | solution.py:502
  156.9 21.6 %copy-start.21 = (bf16[2048,512]{1,0:T(8,128)(2,1)S(1)}, bf16[2048,512]{1,0:T(8,128)(2,1)}, u32[]{:S(2)}) copy-start(bf16[2048,512]{1,0:T(8,128)(2,1)} %down_ref.1) | copy-start | bytes 6291460
  156.9 21.6 %copy-start.22 = (bf16[1024,512]{1,0:T(8,128)(2,1)S(1)}, bf16[1024,512]{1,0:T(8,128)(2,1)}, u32[]{:S(2)}) copy-start(bf16[1024,512]{1,0:T(8,128)(2,1)} %get-tuple-element.50.hidden_ref) | copy-start | bytes 3145732
  158.4 8.7 %collective-permute-start.5 = (bf16[2,16,2048]{2,1,0:T(8,128)(2,1)S(1)}, bf16[2,16,2048]{2,1,0:T(8,128)(2,1)S(1)}, u32[]{:S(2)}, u32[]{:S(2)}) collective-permute-start(bf16[2,16,2048]{2,1,0:T(8,128)(2,1)S(1)} %get-tuple-element.69), channel_id=1, source_target_pairs={{0,8},{1,9},{4,12},{5,13},{2,10},{3,11},{6,14},{7,15},{8,16},{9,17... | collective-permute-start | bytes 393224 | tf_op jit(solution)/shard_map/ppermute | solution.py:496
  160.0 13.1 %collective-permute-start.6 = (bf16[2,16,2048]{2,1,0:T(8,128)(2,1)S(1)}, bf16[2,16,2048]{2,1,0:T(8,128)(2,1)S(1)}, u32[]{:S(2)}, u32[]{:S(2)}) collective-permute-start(bf16[2,16,2048]{2,1,0:T(8,128)(2,1)S(1)} %get-tuple-element.70), channel_id=1, source_target_pairs={{0,16},{1,17},{4,20},{5,21},{2,18},{3,19},{6,22},{7,23},{8,24},{9,... | collective-permute-start | bytes 393224 | tf_op jit(solution)/shard_map/ppermute | solution.py:496
  162.2 10.9 %collective-permute-start.7 = (bf16[2,16,2048]{2,1,0:T(8,128)(2,1)S(1)}, bf16[2,16,2048]{2,1,0:T(8,128)(2,1)S(1)}, u32[]{:S(2)}, u32[]{:S(2)}) collective-permute-start(bf16[2,16,2048]{2,1,0:T(8,128)(2,1)S(1)} %get-tuple-element.71), channel_id=1, source_target_pairs={{0,24},{1,25},{4,28},{5,29},{2,26},{3,27},{6,30},{7,31},{8,0},{9,1... | collective-permute-start | bytes 393224 | tf_op jit(solution)/shard_map/ppermute | solution.py:496
  173.2 10.8 %collective-permute-start.8 = (bf16[2,8,2048]{2,1,0:T(8,128)(2,1)S(1)}, bf16[2,8,2048]{2,1,0:T(8,128)(2,1)S(1)}, u32[]{:S(2)}, u32[]{:S(2)}) collective-permute-start(bf16[2,8,2048]{2,1,0:T(8,128)(2,1)S(1)} %get-tuple-element.73), channel_id=1, source_target_pairs={{0,128},{1,129},{4,132},{5,133},{2,130},{3,131},{6,134},{7,135},{8... | collective-permute-start | bytes 196616 | tf_op jit(solution)/shard_map/ppermute | solution.py:717
  177.1 7.5 %collective-permute-start.14 = (bf16[1056,128]{1,0:T(8,128)(2,1)S(1)}, bf16[1056,128]{1,0:T(8,128)(2,1)S(1)}, u32[]{:S(2)}, u32[]{:S(2)}) collective-permute-start(bf16[1056,128]{1,0:T(8,128)(2,1)S(1)} %add_convert_fusion.2), channel_id=1, source_target_pairs={{0,2},{2,0},{1,3},{3,1},{4,6},{6,4},{5,7},{7,5},{8,10},{10,8},{9,1... | collective-permute-start | bytes 811016 | tf_op jit(solution)/shard_map/ppermute | solution.py:503
  184.0 3.8 %collective-permute-start.9 = (bf16[2,4,2048]{2,1,0:T(4,128)(2,1)S(1)}, bf16[2,4,2048]{2,1,0:T(4,128)(2,1)S(1)}, u32[]{:S(2)}, u32[]{:S(2)}) collective-permute-start(bf16[2,4,2048]{2,1,0:T(4,128)(2,1)S(1)} %get-tuple-element.75), channel_id=1, source_target_pairs={{0,64},{1,65},{4,68},{5,69},{2,66},{3,67},{6,70},{7,71},{8,72},{9,... | collective-permute-start | bytes 98312 | tf_op jit(solution)/shard_map/ppermute | solution.py:719
  187.8 8.2 %copy-start.1 = (bf16[1,1024,512]{2,1,0:T(8,128)(2,1)S(1)}, bf16[1,1024,512]{2,1,0:T(8,128)(2,1)}, u32[]{:S(2)}) copy-start(bf16[1,1024,512]{2,1,0:T(8,128)(2,1)} %param.11) | copy-start | bytes 3145732
  187.8 8.2 %copy-start.4 = (bf16[1024,512]{1,0:T(8,128)(2,1)S(1)}, bf16[1024,512]{1,0:T(8,128)(2,1)}, u32[]{:S(2)}) copy-start(bf16[1024,512]{1,0:T(8,128)(2,1)} %get-tuple-element.59.grad_hidden_ref) | copy-start | bytes 3145732
  187.8 8.2 %copy-start.5 = (f32[1024,512]{1,0:T(8,128)S(1)}, f32[1024,512]{1,0:T(8,128)}, u32[]{:S(2)}) copy-start(f32[1024,512]{1,0:T(8,128)} %get-tuple-element.62.gate_term_ref) | copy-start | bytes 6291460
  187.8 8.2 %copy-start.8 = (bf16[8,128,128]{2,1,0:T(8,128)(2,1)S(1)}, bf16[8,128,128]{2,1,0:T(8,128)(2,1)}, u32[]{:S(2)}) copy-start(bf16[8,128,128]{2,1,0:T(8,128)(2,1)} %factor_ref.3) | copy-start | bytes 786436
  187.9 12.0 %collective-permute-start.10 = (bf16[2,2,2048]{2,1,0:T(2,128)(2,1)S(1)}, bf16[2,2,2048]{2,1,0:T(2,128)(2,1)S(1)}, u32[]{:S(2)}, u32[]{:S(2)}) collective-permute-start(bf16[2,2,2048]{2,1,0:T(2,128)(2,1)S(1)} %get-tuple-element.77), channel_id=1, source_target_pairs={{0,32},{1,33},{4,36},{5,37},{2,34},{3,35},{6,38},{7,39},{8,40},{9,... | collective-permute-start | bytes 49160 | tf_op jit(solution)/shard_map/ppermute | solution.py:721
  191.8 8.1 %collective-permute-start.11 = (bf16[1024,128]{1,0:T(8,128)(2,1)S(1)}, bf16[1024,128]{1,0:T(8,128)(2,1)S(1)}, u32[]{:S(2)}, u32[]{:S(2)}) collective-permute-start(bf16[1024,128]{1,0:T(8,128)(2,1)S(1)} %shard_map.178), channel_id=1, source_target_pairs={{0,1},{1,0},{2,3},{3,2},{4,5},{5,4},{6,7},{7,6},{8,9},{9,8},{10,11... | collective-permute-start | bytes 786440 | tf_op jit(solution)/shard_map/ppermute | solution.py:502
  199.9 9.5 %collective-permute-start.12 = (bf16[1024,128]{1,0:T(8,128)(2,1)S(1)}, bf16[1024,128]{1,0:T(8,128)(2,1)S(1)}, u32[]{:S(2)}, u32[]{:S(2)}) collective-permute-start(bf16[1024,128]{1,0:T(8,128)(2,1)S(1)} %add_convert_fusion.4), channel_id=1, source_target_pairs={{0,2},{2,0},{1,3},{3,1},{4,6},{6,4},{5,7},{7,5},{8,10},{10,8},{9,1... | collective-permute-start | bytes 786440 | tf_op jit(solution)/shard_map/ppermute | solution.py:503
  (10 other events, 42.6 us)
